TPU v7x, 32 devices: a whole 2x2x4 slice. The times are simulated.
32 devices in a mesh: clip: 2 (over y), slab: 4 (over z), chan: 2 (over x), zs: 2 (over core).
Axes of the slice: x: 2, y: 2, z: 4, core: 2. Of those that a mesh axis runs over, the one named last changes fastest.
Arguments:
- voxels: bfloat16 [32, 200, 16, 128], P(('clip', 'slab', 'chan'), None, 'zs'), parts along dimension 0, may hold values from -6 to 6
- image_feat: bfloat16 [32768, 128], P(('clip', 'slab', 'chan')), parts along dimension 0, may hold values from -6 to 6
- coarse: bfloat16 [16, 100, 8, 128], P(('clip', 'slab', 'chan'), None, 'zs'), parts along dimension 0, may hold values from -6 to 6
- wedge_ids: int32 [32, 200, 1], P(('clip', 'slab', 'chan')), parts along dimension 0, may hold values from 0 to 7; in each aligned block of 400 rows (0 to 399, 400 to 799, ..., all dimensions but the last counted through in order) at most 125 rows name the same one
- hit_block: int32 [32, 200], P(('clip', 'slab', 'chan')), parts along dimension 0, may hold values from 0 to 15
- corners: int32 [8, 16, 200, 16], P('clip', ('slab', 'chan'), None, 'zs'), parts along dimension 0, may hold values from 0 to 127
- bilinear: bfloat16 [8, 16, 200, 16], P('clip', ('slab', 'chan'), None, 'zs'), parts along dimension 0, may hold values from 0 to 1
- w_point: bfloat16 [128, 4], replicated, may hold values from -0.5 to 0.5
- w_out: bfloat16 [128, 128], replicated, may hold values from -0.5 to 0.5
- w_conv: bfloat16 [3, 3, 3, 128, 128], replicated, may hold values from -0.109375 to 0.109375
- w_up: bfloat16 [4, 4, 2, 128, 128], replicated, may hold values from -0.25 to 0.25
Outputs:
- refined: bfloat16 [32, 200, 16, 128], P(('clip', 'slab', 'chan'), None, 'zs'), parts along dimension 0
There are 2 independent parts, one for each index of `clip`. A program takes and returns all parts, laid end to end along the dimension named above; an argument that names none is the same for every part. Nothing has to cross between parts.
Inputs may be any that keep to these rules, and one draw needn't show every extreme that they name: `wedge_ids`: the 400 pillars of one x-slab (aligned blocks of rows) name any one wedge at most 125 times.
All inputs are finite; a program needn't handle non-finite values.
Results may differ from a plain program's by a relative error of at most 0.0051.
Values may be sent and summed in bfloat16 or wider, within the bound.
A program may use at most 128 MiB of HBM per device.

v0:
```python
import math

import jax
import jax.numpy as jnp
from jax import lax
from jax.sharding import PartitionSpec as P

KB = 128


def padded_2(x, sides, width):
    for axis, dim in sides:
        count, length = (lax.axis_size(axis), x.shape[dim])
        up = [(i, (i + 1) % count) for i in range(count - 1)]
        down = [(j, i) for i, j in up]
        last = lax.slice_in_dim(x, length - width, length, axis=dim)
        initial = lax.slice_in_dim(x, 0, width, axis=dim)
        before = lax.ppermute(last, axis, up)
        after = lax.ppermute(initial, axis, down)
        x = jnp.concatenate([before, x, after], axis=dim)
    return x


def passed_along(block, axis, distance):
    devices = range(lax.axis_size(axis))
    route = [(i - distance, i) for i in devices if i - distance in devices]
    return lax.ppermute(block, axis, route)


def gather_sum(table, weights, corner_idx, block_idx):
    wedges, slots, points, layers = weights.shape
    pixels = KB
    channels = table.shape[1]
    blocks_table = table.reshape(-1, pixels, channels)
    group = math.gcd(wedges, 8)
    steps_count = wedges // group
    lanes = jnp.arange(pixels, dtype=jnp.int32)

    def one_group(inputs):
        weight_g, corner_g, block_g = inputs
        picked = jnp.take(blocks_table, block_g, axis=0)
        total = jnp.zeros((group, slots, layers, channels), jnp.float32)
        for corner in range(points):
            match = (corner_g[:, :, corner, :, None] == lanes).astype(jnp.bfloat16)
            onehot = weight_g[:, :, corner, :, None] * match
            total = total + jnp.einsum(
                "gsqk,gskc->gsqc", onehot, picked, preferred_element_type=jnp.float32
            )
        return total.astype(jnp.bfloat16)

    result = lax.map(
        one_group,
        (
            weights.reshape((steps_count, group) + weights.shape[1:]),
            corner_idx.reshape((steps_count, group) + corner_idx.shape[1:]),
            block_idx.reshape(steps_count, group, slots),
        ),
    )
    return result.reshape(wedges, slots, layers, channels)


def spread_coarse(source, up_matrix, channels):
    rows_c, cols_c, layers_c = (source.shape[0], source.shape[1], source.shape[2])
    terms = jnp.dot(source.reshape(-1, channels), up_matrix, preferred_element_type=jnp.float32)
    terms = terms.reshape(rows_c, cols_c, layers_c, 4, 4, 2, channels)
    padded_terms = jnp.pad(terms, ((1, 1), (1, 1), (0, 0), (0, 0), (0, 0), (0, 0), (0, 0)))
    parity_x = []
    for par_x in range(2):
        parity_y = []
        for par_y in range(2):
            parity_z = []
            for par_z in range(2):
                block = jnp.zeros((rows_c + 1, cols_c + 1, layers_c, channels), jnp.float32)
                for step_x in range(2):
                    for step_y in range(2):
                        block = (
                            block
                            + padded_terms[
                                1 - step_x : 2 - step_x + rows_c,
                                1 - step_y : 2 - step_y + cols_c,
                                :,
                                par_x + 2 * step_x,
                                par_y + 2 * step_y,
                                par_z,
                            ]
                        )
                parity_z.append(block)
            parity_y.append(jnp.stack(parity_z, axis=3))
        parity_x.append(jnp.stack(parity_y, axis=2))
    woven = jnp.stack(parity_x, axis=1)
    return woven.reshape(2 * rows_c + 2, 2 * cols_c + 2, 2 * layers_c, channels)


def body(
    voxels,
    image_feat,
    coarse,
    wedge_ids,
    hit_block,
    corners,
    bilinear,
    w_point,
    w_out,
    w_conv,
    w_up,
):
    rows_x, cols_y, layers_z, channels = voxels.shape
    points = corners.shape[0]
    wedges = lax.axis_size(("slab", "chan"))
    capacity = max(2, 5 * rows_x * cols_y // (2 * wedges))
    pillars = rows_x * cols_y
    target = wedge_ids.reshape(pillars)
    member = (target[:, None] == jnp.arange(wedges, dtype=jnp.int32)[None, :]).astype(jnp.int32)
    earlier = jnp.cumsum(member, axis=0) - member
    slot_of = target * capacity + jnp.sum(earlier * member, axis=1)
    block_rows = hit_block.reshape(pillars)
    corner_rows = jnp.transpose(corners.reshape(points, pillars, layers_z), (1, 0, 2))
    bil_rows = jnp.transpose(bilinear.reshape(points, pillars, layers_z), (1, 0, 2))
    query_rows = voxels.reshape(pillars, layers_z, channels)

    def place(values):
        buffer = jnp.zeros((wedges * capacity,) + values.shape[1:], values.dtype)
        return buffer.at[slot_of].set(values).reshape((wedges, capacity) + values.shape[1:])

    feat_in = lax.all_to_all(
        place(query_rows), ("slab", "chan"), split_axis=0, concat_axis=0, tiled=True
    )
    bil_in = lax.all_to_all(
        place(bil_rows), ("slab", "chan"), split_axis=0, concat_axis=0, tiled=True
    )
    corner_in = lax.all_to_all(
        place(corner_rows), ("slab", "chan"), split_axis=0, concat_axis=0, tiled=True
    )
    block_in = lax.all_to_all(
        place(block_rows), ("slab", "chan"), split_axis=0, concat_axis=0, tiled=True
    )
    logits_in = jnp.einsum("wsqc,cp->wspq", feat_in, w_point, preferred_element_type=jnp.float32)
    weights_in = (bil_in.astype(jnp.float32) * jax.nn.sigmoid(logits_in)).astype(jnp.bfloat16)
    sampled = gather_sum(image_feat, weights_in, corner_in, block_in)
    returned = lax.all_to_all(sampled, ("slab", "chan"), split_axis=0, concat_axis=0, tiled=True)
    flat_back = returned.reshape(wedges * capacity, layers_z, channels)
    mine = jnp.take(flat_back, slot_of, axis=0)
    mixed = jnp.dot(mine.reshape(-1, channels), w_out, preferred_element_type=jnp.float32)
    attended = (voxels.astype(jnp.float32) + mixed.reshape(voxels.shape)).astype(jnp.bfloat16)
    padded = padded_2(attended, ((("slab", "chan"), 0), ("zs", 2)), 1)
    padded = jnp.pad(padded, ((0, 0), (1, 1), (0, 0), (0, 0)))
    stacked = jnp.concatenate(
        [padded[:, :, shift_z : shift_z + layers_z, :] for shift_z in range(3)], axis=3
    )
    kernel = w_conv.reshape(3, 3, 3 * channels, channels)
    conv = jnp.zeros((rows_x * cols_y * layers_z, channels), jnp.float32)
    for shift_x in range(3):
        for shift_y in range(3):
            window = stacked[shift_x : shift_x + rows_x, shift_y : shift_y + cols_y].reshape(
                -1, 3 * channels
            )
            conv = conv + jnp.dot(
                window, kernel[shift_x, shift_y], preferred_element_type=jnp.float32
            )
    conv = conv.reshape(rows_x, cols_y, layers_z, channels)
    up_matrix = jnp.transpose(w_up, (3, 0, 1, 2, 4)).reshape(channels, 32 * channels)
    buffer = spread_coarse(coarse, up_matrix, channels)[:, 1 : 1 + cols_y]
    from_left = passed_along(
        buffer[rows_x + 1 : rows_x + 2].astype(jnp.bfloat16), ("slab", "chan"), 1
    ).astype(jnp.float32)
    from_right = passed_along(buffer[0:1].astype(jnp.bfloat16), ("slab", "chan"), -1).astype(
        jnp.float32
    )
    upsampled = buffer[1 : 1 + rows_x]
    upsampled = upsampled.at[0:1].add(from_left)
    upsampled = upsampled.at[rows_x - 1 : rows_x].add(from_right)
    refined = attended.astype(jnp.float32) + jnp.maximum(conv, 0.0) + upsampled
    return refined.astype(jnp.bfloat16)


def solution(mesh):
    return jax.shard_map(
        body,
        mesh=mesh,
        in_specs=(
            P(("clip", "slab", "chan"), None, "zs", None),
            P(("clip", "slab", "chan"), None),
            P(("clip", "slab", "chan"), None, "zs", None),
            P(("clip", "slab", "chan"), None, None),
            P(("clip", "slab", "chan"), None),
            P("clip", ("slab", "chan"), None, "zs"),
            P("clip", ("slab", "chan"), None, "zs"),
            P(),
            P(),
            P(),
            P(),
        ),
        out_specs=P(("clip", "slab", "chan"), None, "zs", None),
        check_vma=False,
    )
```

profile of v0, /device:TPU:0, one launch (start us, length us, event | category | flops | bytes accessed | tf_op | source)
XLA Modules:
  0.0 359.4 jit_solution(3247736524055206904)
XLA Ops:
  0.0 1.3 fusion.123
  1.4 1.1 reduce-window.6
  3.8 2.9 scatter_custom_fusion.3
  7.4 7.3 %all-to-all-start.3 = ((s32[8,1,125]{2,1,0:T(1,128)}), s32[8,1,125]{2,1,0:T(1,128)S(1)}, u32[]{:S(2)}, u32[]{:S(2)}) async-start(s32[8,1,125]{2,1,0:T(1,128)} %all_to_all.25), calls=%async_computation.3 | async-start | bytes 8192 | tf_op jit(solution)/shard_map/all_to_all | solution.py:134
  16.3 12.3 %scatter_fusion = s32[1000,4,8]{2,1,0:T(4,128)S(1)} fusion(s32[1000,4,8]{2,1,0:T(4,128)S(1)} %broadcast_in_dim.50, s32[400]{0:T(512)S(1)} %bitcast.378, s32[400,4,8]{2,1,0:T(4,128)S(1)} %copy.141), kind=kCustom, calls=%fused_computation.2 | custom fusion | bytes 155200 | tf_op jit(solution)/shard_map/scatter | solution.py:123
  28.6 1.4 copy.142
  30.6 6.0 %all-to-all-start = ((s32[8,125,4,8]{1,3,2,0:T(8,128)}), s32[8,125,4,8]{1,3,2,0:T(8,128)S(1)}, u32[]{:S(2)}, u32[]{:S(2)}) async-start(s32[8,125,4,8]{1,3,2,0:T(8,128)} %copy.142), calls=%async_computation | async-start | bytes 262144 | tf_op jit(solution)/shard_map/all_to_all | solution.py:131
  36.6 1.6 broadcast_in_dim.52
  38.2 38.1 %scatter_fusion.2 = bf16[1000,8,128]{2,1,0:T(8,128)(2,1)} fusion(bf16[1000,8,128]{2,1,0:T(8,128)(2,1)} %broadcast_in_dim.52, s32[400]{0:T(512)S(1)} %bitcast.379, bf16[400,8,128]{2,1,0:T(8,128)(2,1)S(1)} %bitcast.364), kind=kCustom, calls=%fused_computation.4 | custom fusion | bytes 2459200 | tf_op jit(solution)/shard_map/scatter | solution.py:123
  76.3 6.0 %all-to-all-start.2 = ((bf16[8,125,8,128]{3,2,1,0:T(8,128)(2,1)}), bf16[8,125,8,128]{3,2,1,0:T(8,128)(2,1)S(1)}, u32[]{:S(2)}, u32[]{:S(2)}) async-start(bf16[8,125,8,128]{3,2,1,0:T(8,128)(2,1)} %bitcast.11), calls=%async_computation.2 | async-start | bytes 4096000 | tf_op jit(solution)/shard_map/all_to_all | solution.py:125
  83.8 1.0 copy.145
  84.8 1.3 broadcast_in_dim.51
  86.0 39.6 %scatter_fusion.1 = bf16[1000,4,8]{2,1,0:T(4,128)(2,1)} fusion(bf16[1000,4,8]{2,1,0:T(4,128)(2,1)} %broadcast_in_dim.51, s32[400]{0:T(512)} %bitcast.380, bf16[400,4,8]{2,1,0:T(4,128)(2,1)} %copy.145), kind=kCustom, calls=%fused_computation.3 | custom fusion | bytes 78400 | tf_op jit(solution)/shard_map/scatter | solution.py:123
  125.7 2.1 copy.146
  127.8 20.7 %gather_fusion = bf16[1000,128,128]{2,1,0:T(8,128)(2,1)} fusion(bf16[16,128,128]{2,1,0:T(8,128)(2,1)S(1)} %bitcast.341, s32[1024]{0:T(1024)S(1)} %pad_clamp_fusion.1), kind=kCustom, calls=%fused_computation | custom fusion | bytes 65540000 | tf_op jit(solution)/shard_map/while/body/eval_jaxpr/jit(_take)/gather | solution.py:41
  148.6 1.0 copy.153
  149.6 1.0 copy.151
  150.6 1.0 copy.149
  151.7 1.0 copy.143
  152.7 6.1 %all-to-all-start.1 = ((bf16[8,125,4,8]{1,3,2,0:T(8,128)(2,1)}), bf16[8,125,4,8]{1,3,2,0:T(8,128)(2,1)S(1)}, u32[]{:S(2)}, u32[]{:S(2)}) async-start(bf16[8,125,4,8]{1,3,2,0:T(8,128)(2,1)} %copy.146), calls=%async_computation.1 | async-start | bytes 131072 | tf_op jit(solution)/shard_map/all_to_all | solution.py:128
  158.8 10.4 %fusion.111 = f32[8,125,8,4]{2,3,1,0:T(4,128)} fusion(bf16[8,125,8,128]{3,2,1,0:T(8,128)(2,1)S(1)} %all-to-all-done.2, bf16[128,4]{0,1:T(4,128)(2,1)S(1)} %copy-done.30), kind=kOutput, calls=%fused_computation.210 | convolution fusion | flops 8192000 | bytes 2177024 | tf_op jit(solution)/shard_map/wsqc,cp->wspq/dot_general | solution.py:137
  169.2 1.9 copy.147
  171.4 0.9 copy.152
  172.3 0.9 copy.150
  173.4 18.6 %fusion = f32[8,125,8,128]{3,2,1,0:T(8,128)} fusion(bf16[8,125,128,128]{3,2,1,0:T(8,128)(2,1)} %bitcast.342, pred[8,125]{1,0:T(8,128)(4,1)S(1)} %compare_and_fusion, s32[8,125,8]{2,1,0:T(8,128)S(1)} %copy-done.19, bf16[8,125,8]{2,1,0:T(8,128)(2,1)S(1)} %copy.154), kind=kOutput, calls=%fused_computation.39 | convolution fusion | flops 280576000 | bytes 36913000 | tf_op jit(solution)/shard_map/while/body/eval_jaxpr/gsqk,gskc->gsqc/dot_general | solution.py:46
  192.1 18.0 %fusion.1 = f32[8,125,8,128]{3,2,1,0:T(8,128)} fusion(bf16[8,125,128,128]{3,2,1,0:T(8,128)(2,1)} %bitcast.343, pred[8,125]{1,0:T(8,128)(4,1)S(1)} %compare_and_fusion, s32[8,125,8]{2,1,0:T(8,128)S(1)} %copy-done.18, bf16[8,125,8]{2,1,0:T(8,128)(2,1)} %copy.152), kind=kOutput, calls=%fused_computation.40 | convolution fusion | flops 280576000 | bytes 36913000 | tf_op jit(solution)/shard_map/while/body/eval_jaxpr/gsqk,gskc->gsqc/dot_general | solution.py:46
  210.2 12.2 %fusion.2 = f32[8,125,8,128]{3,2,1,0:T(8,128)} fusion(bf16[8,125,128,128]{3,2,1,0:T(8,128)(2,1)S(1)} %bitcast.347, pred[8,125]{1,0:T(8,128)(4,1)S(1)} %compare_and_fusion, s32[8,125,8]{2,1,0:T(8,128)S(1)} %copy-done.17, bf16[8,125,8]{2,1,0:T(8,128)(2,1)} %copy.150), kind=kOutput, calls=%fused_computation.41 | convolution fusion | flops 280576000 | bytes 36913000 | tf_op jit(solution)/shard_map/while/body/eval_jaxpr/gsqk,gskc->gsqc/dot_general | solution.py:46
  222.4 17.9 %add_convert_fusion = bf16[8,125,8,128]{3,2,1,0:T(8,128)(2,1)} fusion(f32[8,125,8,128]{3,2,1,0:T(8,128)} %fusion, f32[8,125,8,128]{3,2,1,0:T(8,128)} %fusion.1, f32[8,125,8,128]{3,2,1,0:T(8,128)} %fusion.2, bf16[8,125,128,128]{3,2,1,0:T(8,128)(2,1)} %bitcast.344, pred[8,125]{1,0:T(8,128)(4,1)S(1)} %compare_and_fusion, s32[8,125,8]{2,1,0:T(8,128)S(1)} %copy-done.16, ...), kind=kOutput, calls=%fused_computation.60 | convolution fusion | flops 284672000 | bytes 47153000 | tf_op jit(solution)/shard_map/while/body/eval_jaxpr/gsqk,gskc->gsqc/dot_general | solution.py:46
  240.3 6.1 %all-to-all-start.4 = ((bf16[8,125,8,128]{3,2,1,0:T(8,128)(2,1)}), bf16[8,125,8,128]{3,2,1,0:T(8,128)(2,1)}, u32[]{:S(2)}, u32[]{:S(2)}) async-start(bf16[8,125,8,128]{3,2,1,0:T(8,128)(2,1)} %add_convert_fusion), calls=%async_computation.4 | async-start | bytes 4096000 | tf_op jit(solution)/shard_map/all_to_all | solution.py:140
  246.4 1.6 copy.155
  248.0 1.1 convolution_bitcast_fusion
  250.4 2.6 copy.185
  253.3 1.4 copy-done.2
  254.7 4.0 %collective-permute-start.4 = (bf16[1,200,8,128]{3,2,1,0:T(8,128)(2,1)S(1)}, bf16[1,200,8,128]{3,2,1,0:T(8,128)(2,1)S(1)}, u32[]{:S(2)}, u32[]{:S(2)}) collective-permute-start(bf16[1,200,8,128]{3,2,1,0:T(8,128)(2,1)S(1)} %get-tuple-element.72), channel_id=1, source_target_pairs={{0,2},{2,4},{4,6},{6,8},{8,10},{10,12},{12,14},{1,3},{3,5},{5,7},{... | collective-permute-start | bytes 1228808 | tf_op jit(solution)/shard_map/ppermute | solution.py:27
  258.8 32.9 %all-to-all-done.4 = bf16[8,125,8,128]{3,2,1,0:T(8,128)(2,1)} async-done(((bf16[8,125,8,128]{3,2,1,0:T(8,128)(2,1)}), bf16[8,125,8,128]{3,2,1,0:T(8,128)(2,1)}, u32[]{:S(2)}, u32[]{:S(2)}) %all-to-all-start.4) | async-done | bytes 2048032 | tf_op jit(solution)/shard_map/all_to_all | solution.py:140
  291.7 2.6 gather_fusion.1
  295.2 5.1 %collective-permute-start = (bf16[1,200,8,128]{3,2,1,0:T(8,128)(2,1)S(1)}, bf16[1,200,8,128]{3,2,1,0:T(8,128)(2,1)S(1)}, u32[]{:S(2)}, u32[]{:S(2)}) collective-permute-start(bf16[1,200,8,128]{3,2,1,0:T(8,128)(2,1)S(1)} %get-tuple-element.75), channel_id=1, source_target_pairs={{0,2},{2,4},{4,6},{6,8},{8,10},{10,12},{12,14},{1,3},{3,5},{5,7},{... | collective-permute-start | bytes 1228808 | tf_op jit(solution)/shard_map/ppermute | solution.py:18
  300.4 1.3 collective-permute-start.1
  301.7 1.3 collective-permute-start.5
  303.2 22.6 %collective-permute-done = bf16[1,200,8,128]{3,2,1,0:T(8,128)(2,1)S(1)} collective-permute-done((bf16[1,200,8,128]{3,2,1,0:T(8,128)(2,1)S(1)}, bf16[1,200,8,128]{3,2,1,0:T(8,128)(2,1)S(1)}, u32[]{:S(2)}, u32[]{:S(2)}) %collective-permute-start) | collective-permute-done | bytes 409632 | tf_op jit(solution)/shard_map/ppermute | solution.py:18
  326.3 1.3 collective-permute-start.2
  327.7 1.6 collective-permute-start.3
  329.4 1.2 copy-done.4
  331.3 3.5 select_maximum_fusion
  336.4 6.9 %fusion.124 = (bf16[2,200,8,384]{3,2,1,0:T(8,128)(2,1)}, bf16[2,200,8,384]{3,2,1,0:T(8,128)(2,1)}, bf16[2,200,8,384]{3,2,1,0:T(8,128)(2,1)}, bf16[2,200,8,384]{3...) fusion(bf16[4,202,8,384]{3,2,1,0:T(8,128)(2,1)S(1)} %pad_maximu, ...), kind=kLoop, calls=%fused_computation.224 | loop fusion | bytes 44236800 | tf_op jit(solution)/shard_map/slice | solution.py:154
  347.5 0.9 copy-done.11
  349.2 0.9 copy-done.10
  358.3 1.1 add_convert_fusion.1
  (140 shorter events, 25.2 us)
Async XLA Ops:
  0.0 127.8 %copy-start = (bf16[2048,128]{1,0:T(8,128)(2,1)S(1)}, bf16[2048,128]{1,0:T(8,128)(2,1)}, u32[]{:S(2)}) copy-start(bf16[2048,128]{1,0:T(8,128)(2,1)} %param.16) | copy-start | bytes 1572868
  3.0 11.7 %copy-start.27 = (s32[400]{0:T(512)}, s32[400]{0:T(512)S(1)}, u32[]{:S(2)}) copy-start(s32[400]{0:T(512)S(1)} %fusion.108) | copy-start | bytes 4804
  3.8 34.4 %copy-start.21 = (s32[400,1]{0,1:T(1,128)}, s32[400,1]{0,1:T(1,128)S(1)}, u32[]{:S(2)}) copy-start(s32[400,1]{0,1:T(1,128)S(1)} %compare_select_fusion) | copy-start | bytes 4804
  7.4 22.6 %all-to-all-start.3 = ((s32[8,1,125]{2,1,0:T(1,128)}), s32[8,1,125]{2,1,0:T(1,128)S(1)}, u32[]{:S(2)}, u32[]{:S(2)}) async-start(s32[8,1,125]{2,1,0:T(1,128)} %all_to_all.25), calls=%async_computation.3 | async-start | bytes 8192 | tf_op jit(solution)/shard_map/all_to_all | solution.py:134
  28.6 9.6 %copy-start.14 = (bf16[2,200,8,128]{3,2,1,0:T(8,128)(2,1)S(1)}, bf16[2,200,8,128]{3,2,1,0:T(8,128)(2,1)}, u32[]{:S(2)}) copy-start(bf16[2,200,8,128]{3,2,1,0:T(8,128)(2,1)} %param.15) | copy-start | bytes 2457604
  30.6 45.6 %all-to-all-start = ((s32[8,125,4,8]{1,3,2,0:T(8,128)}), s32[8,125,4,8]{1,3,2,0:T(8,128)S(1)}, u32[]{:S(2)}, u32[]{:S(2)}) async-start(s32[8,125,4,8]{1,3,2,0:T(8,128)} %copy.142), calls=%async_computation | async-start | bytes 262144 | tf_op jit(solution)/shard_map/all_to_all | solution.py:131
  76.3 6.0 %copy-start.26 = (bf16[4,2,200,8]{2,3,1,0:T(8,128)(2,1)S(1)}, bf16[4,2,200,8]{2,3,1,0:T(8,128)(2,1)}, u32[]{:S(2)}) copy-start(bf16[4,2,200,8]{2,3,1,0:T(8,128)(2,1)} %param.21) | copy-start | bytes 76804
  76.3 76.4 %all-to-all-start.2 = ((bf16[8,125,8,128]{3,2,1,0:T(8,128)(2,1)}), bf16[8,125,8,128]{3,2,1,0:T(8,128)(2,1)S(1)}, u32[]{:S(2)}, u32[]{:S(2)}) async-start(bf16[8,125,8,128]{3,2,1,0:T(8,128)(2,1)} %bitcast.11), calls=%async_computation.2 | async-start | bytes 4096000 | tf_op jit(solution)/shard_map/all_to_all | solution.py:125
  84.8 43.0 %copy-start.24 = (s32[8,1,125]{2,1,0:T(1,128)S(1)}, s32[8,1,125]{2,1,0:T(1,128)}, u32[]{:S(2)}) copy-start(s32[8,1,125]{2,1,0:T(1,128)} %copy-done.23) | copy-start | bytes 12004
  148.5 10.2 %copy-start.30 = (bf16[128,4]{0,1:T(4,128)(2,1)S(1)}, bf16[128,4]{0,1:T(4,128)(2,1)}, u32[]{:S(2)}) copy-start(bf16[128,4]{0,1:T(4,128)(2,1)} %param.22) | copy-start | bytes 3076
  152.7 18.4 %all-to-all-start.1 = ((bf16[8,125,4,8]{1,3,2,0:T(8,128)(2,1)}), bf16[8,125,4,8]{1,3,2,0:T(8,128)(2,1)S(1)}, u32[]{:S(2)}, u32[]{:S(2)}) async-start(bf16[8,125,4,8]{1,3,2,0:T(8,128)(2,1)} %copy.146), calls=%async_computation.1 | async-start | bytes 131072 | tf_op jit(solution)/shard_map/all_to_all | solution.py:128
  169.2 4.2 %copy-start.19 = (s32[8,125,8]{2,1,0:T(8,128)S(1)}, s32[8,125,8]{2,1,0:T(8,128)}, u32[]{:S(2)}) copy-start(s32[8,125,8]{2,1,0:T(8,128)} %copy.153) | copy-start | bytes 96004
  173.4 18.7 %copy-start.18 = (s32[8,125,8]{2,1,0:T(8,128)S(1)}, s32[8,125,8]{2,1,0:T(8,128)}, u32[]{:S(2)}) copy-start(s32[8,125,8]{2,1,0:T(8,128)} %copy.151) | copy-start | bytes 96004
  173.4 36.7 %slice-start = ((s8[32768000]{0:T(1024)(128)(4,1)}), s8[4194304]{0:T(1024)(128)(4,1)S(1)}, s32[]{:S(2)}) async-start(s8[32768000]{0:T(1024)(128)(4,1)} %bitcast.345), calls=%async_computation.5 | async-start | bytes 8388608
  173.4 36.7 %slice-start.1 = ((s8[32768000]{0:T(1024)(128)(4,1)}), s8[4194304]{0:T(1024)(128)(4,1)S(1)}, s32[]{:S(2)}) async-start(s8[32768000]{0:T(1024)(128)(4,1)} %bitcast.345), calls=%async_computation.6 | async-start | bytes 8388608
  173.4 36.7 %slice-start.2 = ((s8[32768000]{0:T(1024)(128)(4,1)}), s8[4194304]{0:T(1024)(128)(4,1)S(1)}, s32[]{:S(2)}) async-start(s8[32768000]{0:T(1024)(128)(4,1)} %bitcast.345), calls=%async_computation.7 | async-start | bytes 8388608
  173.4 36.7 %slice-start.3 = ((s8[32768000]{0:T(1024)(128)(4,1)}), s8[4194304]{0:T(1024)(128)(4,1)S(1)}, s32[]{:S(2)}) async-start(s8[32768000]{0:T(1024)(128)(4,1)} %bitcast.345), calls=%async_computation.8 | async-start | bytes 8388608
  192.1 18.0 %slice-start.4 = ((s8[32768000]{0:T(1024)(128)(4,1)}), s8[4194304]{0:T(1024)(128)(4,1)S(1)}, s32[]{:S(2)}) async-start(s8[32768000]{0:T(1024)(128)(4,1)} %bitcast.345), calls=%async_computation.9 | async-start | bytes 8388608
  192.1 18.0 %slice-start.5 = ((s8[32768000]{0:T(1024)(128)(4,1)}), s8[4194304]{0:T(1024)(128)(4,1)S(1)}, s32[]{:S(2)}) async-start(s8[32768000]{0:T(1024)(128)(4,1)} %bitcast.345), calls=%async_computation.10 | async-start | bytes 8388608
  192.1 18.0 %slice-start.6 = ((s8[32768000]{0:T(1024)(128)(4,1)}), s8[4194304]{0:T(1024)(128)(4,1)S(1)}, s32[]{:S(2)}) async-start(s8[32768000]{0:T(1024)(128)(4,1)} %bitcast.345), calls=%async_computation.11 | async-start | bytes 8388608
  192.1 18.0 %slice-start.7 = ((s8[32768000]{0:T(1024)(128)(4,1)}), s8[3407872]{0:T(1024)(128)(4,1)S(1)}, s32[]{:S(2)}) async-start(s8[32768000]{0:T(1024)(128)(4,1)} %bitcast.345), calls=%async_computation.12 | async-start | bytes 6815744
  192.1 18.0 %copy-start.17 = (s32[8,125,8]{2,1,0:T(8,128)S(1)}, s32[8,125,8]{2,1,0:T(8,128)}, u32[]{:S(2)}) copy-start(s32[8,125,8]{2,1,0:T(8,128)} %copy.149) | copy-start | bytes 96004
  210.1 12.2 %copy-start.16 = (s32[8,125,8]{2,1,0:T(8,128)S(1)}, s32[8,125,8]{2,1,0:T(8,128)}, u32[]{:S(2)}) copy-start(s32[8,125,8]{2,1,0:T(8,128)} %copy.143) | copy-start | bytes 96004
  240.3 7.8 %copy-start.20 = (bf16[1,100,4,128]{3,2,1,0:T(4,128)(2,1)S(1)}, bf16[1,100,4,128]{3,2,1,0:T(4,128)(2,1)}, u32[]{:S(2)}) copy-start(bf16[1,100,4,128]{3,2,1,0:T(4,128)(2,1)} %param.17) | copy-start | bytes 307204
  240.3 51.4 %all-to-all-start.4 = ((bf16[8,125,8,128]{3,2,1,0:T(8,128)(2,1)}), bf16[8,125,8,128]{3,2,1,0:T(8,128)(2,1)}, u32[]{:S(2)}, u32[]{:S(2)}) async-start(bf16[8,125,8,128]{3,2,1,0:T(8,128)(2,1)} %add_convert_fusion), calls=%async_computation.4 | async-start | bytes 4096000 | tf_op jit(solution)/shard_map/all_to_all | solution.py:140
  253.0 1.7 copy-start.2
  253.0 5.7 %copy-start.28 = (s32[400]{0:T(512)S(1)}, s32[400]{0:T(512)}, u32[]{:S(2)}) copy-start(s32[400]{0:T(512)} %copy-done.27) | copy-start | bytes 4804
  253.0 5.8 %copy-start.22 = (s32[400,1]{0,1:T(1,128)S(1)}, s32[400,1]{0,1:T(1,128)}, u32[]{:S(2)}) copy-start(s32[400,1]{0,1:T(1,128)} %copy-done.21) | copy-start | bytes 4804
  253.0 5.8 %copy-start.29 = (s32[2,200,1]{1,2,0:T(1,128)S(1)}, s32[2,200,1]{1,2,0:T(1,128)}, u32[]{:S(2)}) copy-start(s32[2,200,1]{1,2,0:T(1,128)} %get-tuple-element.85) | copy-start | bytes 4804
  254.7 39.6 %copy-start.25 = (bf16[128,128]{1,0:T(8,128)(2,1)S(1)}, bf16[128,128]{1,0:T(8,128)(2,1)}, u32[]{:S(2)}) copy-start(bf16[128,128]{1,0:T(8,128)(2,1)} %param.23) | copy-start | bytes 98308
  254.7 48.3 %collective-permute-start.4 = (bf16[1,200,8,128]{3,2,1,0:T(8,128)(2,1)S(1)}, bf16[1,200,8,128]{3,2,1,0:T(8,128)(2,1)S(1)}, u32[]{:S(2)}, u32[]{:S(2)}) collective-permute-start(bf16[1,200,8,128]{3,2,1,0:T(8,128)(2,1)S(1)} %get-tuple-element.72), channel_id=1, source_target_pairs={{0,2},{2,4},{4,6},{6,8},{8,10},{10,12},{12,14},{1,3},{3,5},{5,7},{... | collective-permute-start | bytes 1228808 | tf_op jit(solution)/shard_map/ppermute | solution.py:27
  294.3 8.7 %copy-start.3 = (f32[2,2,101,2,4,2,128]{6,5,4,3,2,1,0:T(2,128)S(1)}, f32[2,2,101,2,4,2,128]{6,5,4,3,2,1,0:T(2,128)}, u32[]{:S(2)}) copy-start(f32[2,2,101,2,4,2,128]{6,5,4,3,2,1,0:T(2,128)} %copy-done.2) | copy-start | bytes 9928708
  295.2 30.6 %collective-permute-start = (bf16[1,200,8,128]{3,2,1,0:T(8,128)(2,1)S(1)}, bf16[1,200,8,128]{3,2,1,0:T(8,128)(2,1)S(1)}, u32[]{:S(2)}, u32[]{:S(2)}) collective-permute-start(bf16[1,200,8,128]{3,2,1,0:T(8,128)(2,1)S(1)} %get-tuple-element.75), channel_id=1, source_target_pairs={{0,2},{2,4},{4,6},{6,8},{8,10},{10,12},{12,14},{1,3},{3,5},{5,7},{... | collective-permute-start | bytes 1228808 | tf_op jit(solution)/shard_map/ppermute | solution.py:18
  300.4 25.4 %collective-permute-start.1 = (bf16[1,200,8,128]{3,2,1,0:T(8,128)(2,1)S(1)}, bf16[1,200,8,128]{3,2,1,0:T(8,128)(2,1)S(1)}, u32[]{:S(2)}, u32[]{:S(2)}) collective-permute-start(bf16[1,200,8,128]{3,2,1,0:T(8,128)(2,1)S(1)} %get-tuple-element.76), channel_id=1, source_target_pairs={{2,0},{4,2},{6,4},{8,6},{10,8},{12,10},{14,12},{3,1},{5,3},{7,5},{... | collective-permute-start | bytes 1228808 | tf_op jit(solution)/shard_map/ppermute | solution.py:19
  301.7 27.6 %collective-permute-start.5 = (bf16[1,200,8,128]{3,2,1,0:T(8,128)(2,1)S(1)}, bf16[1,200,8,128]{3,2,1,0:T(8,128)(2,1)S(1)}, u32[]{:S(2)}, u32[]{:S(2)}) collective-permute-start(bf16[1,200,8,128]{3,2,1,0:T(8,128)(2,1)S(1)} %get-tuple-element.71), channel_id=1, source_target_pairs={{2,0},{4,2},{6,4},{8,6},{10,8},{12,10},{14,12},{3,1},{5,3},{7,5},{... | collective-permute-start | bytes 1228808 | tf_op jit(solution)/shard_map/ppermute | solution.py:27
  326.3 3.1 collective-permute-start.2
  327.7 3.6 %collective-permute-start.3 = (bf16[4,200,1,128]{3,2,1,0:T(2,128)(2,1)S(1)}, bf16[4,200,1,128]{3,2,1,0:T(2,128)(2,1)S(1)}, u32[]{:S(2)}, u32[]{:S(2)}) collective-permute-start(bf16[4,200,1,128]{3,2,1,0:T(2,128)(2,1)S(1)} %get-tuple-element.74), channel_id=1, source_target_pairs={{1,0},{3,2},{5,4},{7,6},{9,8},{11,10},{13,12},{15,14},{17,16},{19,... | collective-permute-start | bytes 614408 | tf_op jit(solution)/shard_map/ppermute | solution.py:19
  336.4 6.9 %copy-start.15 = (bf16[3,3,3,128,128]{4,3,2,1,0:T(8,128)(2,1)S(1)}, bf16[3,3,3,128,128]{4,3,2,1,0:T(8,128)(2,1)}, u32[]{:S(2)}) copy-start(bf16[3,3,3,128,128]{4,3,2,1,0:T(8,128)(2,1)} %param.24) | copy-start | bytes 2654212
  343.3 1.7 copy-start.13
  345.0 1.7 copy-start.12
  346.7 1.7 copy-start.11
  348.4 1.7 copy-start.10
  350.1 1.7 copy-start.9
  351.8 1.7 copy-start.8
  353.4 1.7 copy-start.7
  355.1 1.7 copy-start.6
  356.8 1.4 copy-start.5
  357.6 1.7 copy-start.1
  (2 other events, 1.8 us)
where the time goes:
time: 363 us; the launch traced here: 359 us
  local copies, waits for them, and re-layouts  160 us (44%)
  matrix products  86.2 us (24%)
  waiting for transfers between devices  56.2 us (15%)
  starting transfers between devices  46 us (13%)
  other arithmetic  10.3 us (3%)
    scatter x4, local copies, waits for them, and re-layouts, place(): buffer.at[slot_of].set(values)  92.9 us
    dot_general x4, matrix products, one_group(): jnp.einsum('gsqk,gskc->gsqc', onehot, picked, preferred_element_type=jnp....  66.7 us
    all_to_all x1, waiting for transfers between devices, body(): lax.all_to_all(sampled, ('slab', 'chan'), split_axis=0, concat_axis=0, ti...  32.9 us
    ppermute x2, waiting for transfers between devices, padded_2(): before = lax.ppermute(last, axis, up)  22.6 us
    gather x1, local copies, waits for them, and re-layouts, one_group(): picked = jnp.take(blocks_table, block_g, axis=0)  20.7 us
    unnamed x81, local copies, waits for them, and re-layouts  14.1 us
    dot_general x1, matrix products, body(): jnp.einsum('wsqc,cp->wspq', feat_in, w_point, preferred_element_type=jnp....  10.4 us
  transfers between devices with their start and end apart: 11, of which 3 were waited for; matrix products, arithmetic and copies ran while one was open for 41% of the time, Pallas kernels for 0%

commit v1 on v0

v1 whole, which is shorter than its diff:
```python
import functools

import jax
import jax.numpy as jnp
from jax import lax
from jax.experimental import pallas as pl
from jax.experimental.pallas import tpu as pltpu
from jax.sharding import PartitionSpec as P

KB = 128
MESH = pl.DeviceIdType.MESH
F32 = jnp.float32
BF16 = jnp.bfloat16
VMEM = pltpu.VMEM
LIMIT = 56 * 1024 * 1024


def spaces(*kinds):
    return [pl.BlockSpec(memory_space=k) for k in kinds]


def gate_rows(vox, table, w_gate, select, write, rows):
    lanes = lax.broadcasted_iota(jnp.int32, (256, KB), 1).astype(F32)
    for start in range(0, rows, 256):
        size = min(256, rows - start)
        logits = jnp.dot(vox(start, size), w_gate[...], preferred_element_type=F32)
        spread = lax.dot_general(
            table(start, size), select[...], (((0,), (0,)), ((), ())), preferred_element_type=F32
        )
        total = jnp.zeros((size, KB), F32)
        for p in range(4):
            gate = jax.nn.sigmoid(logits[:, p * KB : (p + 1) * KB])
            coef = (spread[:, (4 + p) * KB : (5 + p) * KB] * gate).astype(BF16).astype(F32)
            hit = spread[:, p * KB : (p + 1) * KB] == lanes[:size]
            total = total + jnp.where(hit, coef, 0.0)
        write(start, size, total.astype(BF16))


def collect(
    ns, nc, img, vox, coarse, table, base, w_gate, select, w_up,
    feats, onehot, up, vox_halo, base_halo,
    coarse_halo, table_halo, dup, local_sem,
    z_send, x_send, c_send, recv, c_recv, h_send, h_recv,
):
    clip, s, x, c = [lax.axis_index(a) for a in ("clip", "slab", "chan", "zs")]
    index = s * nc + x
    rows = vox.shape[1]

    def dev(s_, x_, c_):
        return (clip, s_, x_, c_)

    following, previous = index + 1, index - 1
    relations = [
        (s + 1 < ns, dev(s + 1, x, c)),
        (s > 0, dev(s - 1, x, c)),
        (x + 1 < nc, dev(s, x + 1, c)),
        (x > 0, dev(s, x - 1, c)),
        (following < ns * nc, dev(following // nc, following % nc, c)),
        (index > 0, dev(previous // nc, previous % nc, c)),
        (None, dev(s, x, 1 - c)),
    ]
    barrier = pltpu.get_barrier_semaphore()
    expected = 0
    for there, who in relations:
        def greet(who=who):
            pl.semaphore_signal(barrier, inc=1, device_id=who, device_id_type=MESH)
        if there is None:
            greet()
            expected = expected + 1
        else:
            pl.when(there)(greet)
            expected = expected + there.astype(jnp.int32)
    pl.semaphore_wait(barrier, expected)

    def remote(src, dst, ss, rs, who):
        return pltpu.make_async_remote_copy(
            src_ref=src, dst_ref=dst, send_sem=ss, recv_sem=rs, device_id=who, device_id_type=MESH
        )

    keep = pltpu.make_async_copy(img, feats.at[s, x], local_sem)
    keep.start()
    own = img.at[c]

    def part(s_, x_):
        return feats.at[s_, x_, c]

    sides = ((0, following < ns * nc, relations[4][1], 1), (1, index > 0, relations[5][1], 0))

    def halo_copies(side, who, row):
        pairs = (
            (table.at[row], table_halo.at[side]),
            (base.at[row], base_halo.at[side]),
            (coarse, coarse_halo.at[side]),
            (vox.at[row], vox_halo.at[side]),
        )
        return [
            remote(a, b, h_send.at[side, i], h_recv.at[side, i], who)
            for i, (a, b) in enumerate(pairs)
        ]

    for side, there, who, row in sides:
        @pl.when(there)
        def _(side=side, who=who, row=row):
            for copy in halo_copies(side, who, row):
                copy.start()

    def z_copy(item, direction):
        src = part(item, x)
        return remote(src, src, z_send.at[direction, item], recv.at[item, x], dev(s + 1 - 2 * direction, x, c))

    def x_copy(si, xi, direction):
        src = part(si, xi)
        return remote(src, src, x_send.at[direction, si, xi], recv.at[si, xi], dev(s, x + 1 - 2 * direction, c))

    def c_copy(si, xi):
        src = part(si, xi)
        return remote(src, src, c_send.at[si, xi], c_recv.at[si, xi], dev(s, x, 1 - c))

    def first(dst, ss, who):
        return remote(own, dst, ss, recv.at[s, x], who)

    z_ends = ((0, s + 1 < ns), (1, s > 0))
    x_ends = ((0, x + 1 < nc), (1, x > 0))
    for d, there in z_ends:
        @pl.when(there)
        def _(d=d):
            first(part(s, x), z_send.at[d, s], dev(s + 1 - 2 * d, x, c)).start()
    for d, there in x_ends:
        @pl.when(there)
        def _(d=d):
            first(part(s, x), x_send.at[d, s, x], dev(s, x + 1 - 2 * d, c)).start()

    def z_step(k):
        for d, item, there, on in (
            (0, s - k, s - k >= 0, s + 1 < ns),
            (1, s + k, s + k < ns, s > 0),
        ):
            @pl.when(there)
            def _(d=d, item=item, on=on):
                z_copy(item, d).wait_recv()

                @pl.when(on)
                def _():
                    z_copy(item, d).start()

                for e, far in x_ends:
                    @pl.when(far)
                    def _(e=e):
                        x_copy(item, x, e).start()
                c_copy(item, x).start()

    def x_step(k):
        items = ((s, True),) if k == 0 else ((s - k, s - k >= 0), (s + k, s + k < ns))
        for j in range(1, nc):
            for si, there_s in items:
                for d, xi, there_x, on in (
                    (0, x - j, x - j >= 0, x + 1 < nc),
                    (1, x + j, x + j < nc, x > 0),
                ):
                    @pl.when(jnp.logical_and(there_s, there_x))
                    def _(d=d, si=si, xi=xi, on=on):
                        x_copy(si, xi, d).wait_recv()
                        if nc > 2:
                            @pl.when(on)
                            def _():
                                x_copy(si, xi, d).start()
                        c_copy(si, xi).start()

    def gates(row, vox_ref, table_ref, source):
        gate_rows(
            lambda a, n: vox_ref[source, a : a + n, :],
            lambda a, n: table_ref[source, :, a : a + n],
            w_gate, select,
            lambda a, n, v: onehot.__setitem__((row, slice(a, a + n)), v),
            rows,
        )

    def up_rows():
        count = coarse.shape[0]
        double = []
        for side in range(3):
            ref = coarse if side == 2 else coarse_halo.at[side]
            value = ref[...].astype(F32)
            dup[pl.ds(0, count, stride=2), :] = value
            dup[pl.ds(1, count, stride=2), :] = value
            value = dup[...]
            if side < 2:
                value = jnp.where((index > 0) if side == 0 else (following < ns * nc), value, 0.0)
            double.append(value.astype(BF16))
        even = lax.broadcasted_iota(jnp.int32, (2 * count, KB), 0) % 2 == 0
        gap = jnp.zeros((8, KB), F32)
        for px, (near, far, side) in enumerate(((1, 3, 0), (2, 0, 1))):
            lhs = jnp.concatenate([double[2], double[side]], axis=1)

            def tap(b):
                rhs = jnp.concatenate(
                    [jnp.concatenate([w_up[a, b, 0], w_up[a, b, 1]], axis=1) for a in (near, far)],
                    axis=0,
                )
                out = jnp.dot(lhs, rhs, preferred_element_type=F32)
                return jnp.where(even, out[:, :KB], out[:, KB:])

            first_y = tap(1) + jnp.concatenate([gap, tap(3)[:-8]], axis=0)
            up[px, :, 0] = first_y.reshape(-1, 8, KB)
            second_y = tap(2) + jnp.concatenate([tap(0)[8:], gap], axis=0)
            up[px, :, 1] = second_y.reshape(-1, 8, KB)

    gates(1, vox, table, 0)
    if ns > 1:
        z_step(1)
    gates(2, vox, table, 1)
    x_step(0)
    for side, there, row in ((0, index > 0, 0), (1, following < ns * nc, 1)):
        @pl.when(there)
        def _(side=side, row=row):
            for copy in halo_copies(side, relations[4 + side][1], row):
                copy.wait_recv()

        @pl.when(jnp.logical_not(there))
        def _(side=side, row=row):
            table_halo[side] = table[row]
            base_halo[side] = base[row]
            coarse_halo[side] = coarse[...]
            vox_halo[side] = vox[row]
    for k in range(2, ns):
        z_step(k)
        if k == 2:
            up_rows()
        x_step(k - 1)
        if k == 2:
            gates(0, vox_halo, table_halo, 0)
        if k == 3:
            gates(3, vox_halo, table_halo, 1)
    x_step(ns - 1)

    for si in range(ns):
        for xi in range(nc):
            mine = jnp.logical_and(si == s, xi == x)

            @pl.when(jnp.logical_not(mine))
            def _(si=si, xi=xi):
                dst = feats.at[si, xi, 1 - c]
                remote(dst, dst, c_send.at[si, xi], c_recv.at[si, xi], dev(s, x, 1 - c)).wait_recv()
                c_copy(si, xi).wait_send()
    keep.wait()
    for side, there, who, row in sides:
        @pl.when(there)
        def _(side=side, who=who, row=row):
            for copy in halo_copies(side, who, row):
                copy.wait_send()
    for d, there in z_ends:
        for si in range(ns):
            sent = (si <= s) if d == 0 else (si >= s)

            @pl.when(jnp.logical_and(there, sent))
            def _(d=d, si=si):
                z_copy(si, d).wait_send()
    for d, there in x_ends:
        for si in range(ns):
            for xi in range(nc):
                sent = (xi <= x) if d == 0 else (xi >= x)

                @pl.when(jnp.logical_and(there, sent))
                def _(d=d, si=si, xi=xi):
                    x_copy(si, xi, d).wait_send()


def attend(ns, nc, base, feats, onehot, vox, vox_halo, w_out, attended, sampled):
    index = lax.axis_index("slab") * nc + lax.axis_index("chan")
    rows = vox.shape[1]

    def sample(r):
        def pair(i, carry):
            lhs = onehot[r, pl.ds(pl.multiple_of(i * 16, 16), 16), :]
            one = jnp.dot(lhs, feats[base[r, 2 * i]], preferred_element_type=F32)
            two = jnp.dot(lhs, feats[base[r, 2 * i + 1]], preferred_element_type=F32)
            both = jnp.concatenate([one[:8], two[8:]], axis=0)
            sampled[r, pl.ds(pl.multiple_of(i * 16, 16), 16), :] = both.astype(BF16)
            return carry

        lax.fori_loop(0, rows // 16, pair, 0, unroll=10)

    for r in range(4):
        sample(r)
        mixed = jnp.dot(sampled[r], w_out[...], preferred_element_type=F32)
        query = vox[r - 1] if r in (1, 2) else vox_halo[r // 3]
        total = query.astype(F32) + mixed
        if r == 0:
            total = jnp.where(index > 0, total, 0.0)
        if r == 3:
            total = jnp.where(index < ns * nc - 1, total, 0.0)
        attended[r] = total.astype(BF16)


def convolve(attended, up, w_conv, out, wide, rhs, face, face_in, below, above, acc, sems):
    clip, s, x, c = [lax.axis_index(a) for a in ("clip", "slab", "chan", "zs")]
    other = (clip, s, x, 1 - c)
    rows = attended.shape[1]
    count = rows // 8
    barrier = pltpu.get_barrier_semaphore()
    pl.semaphore_signal(barrier, inc=1, device_id=other, device_id_type=MESH)
    for r in range(4):
        below[...] = attended[r].astype(F32)
        edge = jnp.where(c == 0, below[pl.ds(7, count, stride=8), :], below[pl.ds(0, count, stride=8), :])
        face[r, pl.ds(0, count), :] = edge.astype(BF16)
    pl.semaphore_wait(barrier, 1)
    copy = pltpu.make_async_remote_copy(
        src_ref=face, dst_ref=face_in, send_sem=sems.at[0], recv_sem=sems.at[1],
        device_id=other, device_id_type=MESH,
    )
    copy.start()
    for a in range(3):
        for b in range(3):
            rhs[a * 3 * KB : (a + 1) * 3 * KB, b * KB : (b + 1) * KB] = w_conv[a, b]
    for r in range(4):
        wide[:, (3 * r + 1) * KB : (3 * r + 2) * KB] = attended[r]
    copy.wait()
    nothing = jnp.zeros((1, KB), F32)
    for r in range(4):
        value = attended[r].astype(F32)
        edge = face_in[r, pl.ds(0, count), :].astype(F32)
        below[...] = jnp.concatenate([nothing, value[:-1]], axis=0)
        below[pl.ds(0, count, stride=8), :] = jnp.where(c == 1, edge, 0.0)
        above[...] = jnp.concatenate([value[1:], nothing], axis=0)
        above[pl.ds(7, count, stride=8), :] = jnp.where(c == 0, edge, 0.0)
        wide[:, 3 * r * KB : (3 * r + 1) * KB] = below[...].astype(BF16)
        wide[:, (3 * r + 2) * KB : (3 * r + 3) * KB] = above[...].astype(BF16)
    step = rows // 5
    for o in range(2):
        acc[...] = jnp.zeros_like(acc)

        def chunk(i, carry):
            start = pl.multiple_of(i * step, step)
            lhs = wide[pl.ds(start, step), 3 * o * KB : 3 * (o + 3) * KB]
            part = jnp.dot(lhs, rhs[...], preferred_element_type=F32)
            for b in range(3):
                acc[pl.ds(start + 16 - 8 * b, step), :] += part[:, b * KB : (b + 1) * KB]
            return carry

        lax.fori_loop(0, 5, chunk, 0)
        conv = jnp.maximum(acc[8 : 8 + rows, :], 0.0)
        out[o] = (attended[1 + o].astype(F32) + conv + up[o]).astype(BF16)


def body(
    voxels, image_feat, coarse, wedge_ids, hit_block, corners, bilinear, w_point, w_out, w_conv, w_up
):
    ns, nc = lax.axis_size("slab"), lax.axis_size("chan")
    rows_x, cols_y, layers, channels = voxels.shape
    rows = cols_y * layers
    pixels = image_feat.shape[0]
    half = pixels // 2
    blocks = pixels // KB
    vox = voxels.reshape(rows_x, rows, channels)
    small = coarse.reshape(-1, channels)
    both = jnp.concatenate([corners.astype(F32), bilinear.astype(F32)], axis=0)
    table = jnp.transpose(both.reshape(8, rows_x, rows), (1, 0, 2))
    base = wedge_ids[:, :, 0] * blocks + hit_block
    base = jnp.pad(base, ((0, 0), (0, 1024 - cols_y))).reshape(rows_x, 8, 128)
    w_gate = jnp.repeat(w_point, KB, axis=1)
    select = jnp.repeat(jnp.eye(8, dtype=F32), KB, axis=1)
    dma = pltpu.SemaphoreType.DMA
    feats, onehot, up, vox_halo, base_halo = pl.pallas_call(
        functools.partial(collect, ns, nc),
        name="collect",
        out_shape=(
            jax.ShapeDtypeStruct((ns, nc, 2, half, channels), BF16),
            jax.ShapeDtypeStruct((4, rows, KB), BF16),
            jax.ShapeDtypeStruct((2, cols_y // 2, 2, layers, channels), F32),
            jax.ShapeDtypeStruct((2, rows, channels), BF16),
            jax.ShapeDtypeStruct((2, 8, 128), jnp.int32),
        ),
        in_specs=spaces(pl.ANY, *[VMEM] * 7),
        out_specs=tuple(spaces(pl.ANY, *[VMEM] * 4)),
        scratch_shapes=[
            VMEM((2,) + small.shape, BF16),
            VMEM((2, 8, rows), F32),
            VMEM((2 * small.shape[0], channels), F32),
            dma(()),
            dma((2, ns)),
            dma((2, ns, nc)),
            dma((ns, nc)),
            dma((ns, nc)),
            dma((ns, nc)),
            dma((2, 4)),
            dma((2, 4)),
        ],
        compiler_params=pltpu.CompilerParams(
            collective_id=0, has_side_effects=True, vmem_limit_bytes=LIMIT
        ),
    )(image_feat.reshape(2, half, channels), vox, small, table, base, w_gate, select, w_up)
    index = jnp.concatenate([base_halo[:1], base, base_halo[1:]], axis=0).reshape(4, 1024)
    attended = pl.pallas_call(
        functools.partial(attend, ns, nc),
        name="attend",
        out_shape=jax.ShapeDtypeStruct((4, rows, channels), BF16),
        in_specs=spaces(pltpu.SMEM, *[VMEM] * 5),
        out_specs=pl.BlockSpec(memory_space=VMEM),
        scratch_shapes=[VMEM((4, rows, channels), BF16)],
        compiler_params=pltpu.CompilerParams(vmem_limit_bytes=LIMIT),
    )(index, feats.reshape(ns * nc * blocks, KB, channels), onehot, vox, vox_halo, w_out)
    refined = pl.pallas_call(
        convolve,
        name="convolve",
        out_shape=jax.ShapeDtypeStruct((rows_x, rows, channels), BF16),
        in_specs=spaces(VMEM, VMEM, VMEM),
        out_specs=pl.BlockSpec(memory_space=VMEM),
        scratch_shapes=[
            VMEM((rows, 12 * KB), BF16),
            VMEM((9 * KB, 3 * KB), BF16),
            VMEM((4, 208, KB), BF16),
            VMEM((4, 208, KB), BF16),
            VMEM((rows, KB), F32),
            VMEM((rows, KB), F32),
            VMEM((rows + 16, KB), F32),
            dma((2,)),
        ],
        compiler_params=pltpu.CompilerParams(
            collective_id=1, has_side_effects=True, vmem_limit_bytes=LIMIT
        ),
    )(attended, up.reshape(2, rows, channels), w_conv.reshape(3, 3, 3 * channels, channels))
    return refined.reshape(voxels.shape)


def solution(mesh):
    return jax.shard_map(
        body,
        mesh=mesh,
        in_specs=(
            P(("clip", "slab", "chan"), None, "zs", None),
            P(("clip", "slab", "chan"), None),
            P(("clip", "slab", "chan"), None, "zs", None),
            P(("clip", "slab", "chan"), None, None),
            P(("clip", "slab", "chan"), None),
            P("clip", ("slab", "chan"), None, "zs"),
            P("clip", ("slab", "chan"), None, "zs"),
            P(),
            P(),
            P(),
            P(),
        ),
        out_specs=P(("clip", "slab", "chan"), None, "zs", None),
        check_vma=False,
    )
```

time: 363 us -> 96.6 us (0.27)
  the two profiles are of different devices: /device:TPU:0 before, /device:TPU:17 now
where the time goes in v1:
time: 96.6 us; the launch traced here: 96.2 us
  Pallas kernels  85.9 us (89%)
  local copies, waits for them, and re-layouts  7.34 us (8%)
  other arithmetic  2.95 us (3%)
    pallas_call x1, Pallas kernels, body(): pl.pallas_call(functools.partial(collect, ns, nc), name='collect', out_sh...  56.6 us
    pallas_call x1, Pallas kernels, body(): pl.pallas_call(functools.partial(attend, ns, nc), name='attend', out_shap...  16.9 us
    pallas_call x1, Pallas kernels, body(): pl.pallas_call(convolve, name='convolve', out_shape=jax.ShapeDtypeStruct(...  12.3 us
    unnamed x4, local copies, waits for them, and re-layouts  4.17 us

profile of v1, /device:TPU:17, one launch (start us, length us, event | category | flops | bytes accessed | tf_op | source)
XLA Modules:
  0.0 96.2 jit_solution(15733388497807311228)
XLA Ops:
  0.0 0.7 bitcast_add_fusion
  0.7 0.6 copy.26
  1.3 0.7 broadcast_bitcast_fusion.select
  2.0 0.8 copy.17
  2.8 0.8 convert_element_type.9
  3.6 0.8 convert_element_type.10
  4.4 0.2 broadcast_in_dim.6
  4.6 0.7 copy.25
  5.3 0.5 copy.15
  5.8 1.1 %reshape.43 = f32[8,2,1600]{2,0,1:T(8,128)} reshape(f32[8,2,200,8]{3,2,0,1:T(8,128)S(1)} %copy.15) | data formatting | bytes 204800 | tf_op jit(solution)/shard_map/reshape | solution.py:357
  6.9 56.6 %collect.1 = (bf16[4,2,2,1024,128]{4,3,2,1,0:T(8,128)(2,1)}, bf16[4,1600,128]{2,1,0:T(8,128)(2,1)}, f32[2,100,2,8,128]{4,3,2,1,0:T(8,128)}, bf16[2,1600,128]{2,1,0:T(8,128)(2,1)}, s32[2,8,128]{2,1,0:T(8,128)}) custom-call(bf16[2,1024,128]{2,1,0:T(8,128)(2,1)} %bitcast.34, bf16[2,1600,128]{2,1,0:T(8,128)(2,1)} %bitcast.28, bf16[400,128]{1,0:T(8,128)(2,1)} %bitcast.37, ...), custom_call_target="tpu_custom_call" | custom-call | tf_op jit(solution)/shard_map/collect/pallas_call | solution.py:363
  63.5 0.7 fusion.1
  64.2 0.6 pad_add_fusion.base
  64.9 16.9 %attend.1.attended = bf16[4,1600,128]{2,1,0:T(8,128)(2,1)} custom-call(s32[4,1024]{1,0:T(4,128)} %pad_add_fusion.base, bf16[128,128,128]{2,1,0:T(8,128)(2,1)} %bitcast.27, bf16[4,1600,128]{2,1,0:T(8,128)(2,1)} %get-tuple-element.12.onehot, bf16[2,1600,128]{2,1,0:T(8,128)(2,1)} %bitcast.29, bf16[2,1600,128]{2,1,0:T(8,128)(2,1)} %get-tuple-element.13.vox_halo, ...), custom_call_target="tpu_custom_call" | custom-call | tf_op jit(solution)/shard_map/attend/pallas_call | solution.py:393
  81.8 12.3 %convolve.1 = bf16[2,1600,128]{2,1,0:T(8,128)(2,1)} custom-call(bf16[4,1600,128]{2,1,0:T(8,128)(2,1)} %attend.1.attended, f32[2,1600,128]{2,1,0:T(8,128)} %bitcast.31, bf16[3,3,384,128]{3,2,1,0:T(8,128)(2,1)} %bitcast.32), custom_call_target="tpu_custom_call" | custom-call | tf_op jit(solution)/shard_map/convolve/pallas_call | solution.py:402
  94.1 2.1 %copy.28 = bf16[2,200,8,128]{3,2,1,0:T(8,128)(2,1)} copy(bf16[2,200,8,128]{3,2,1,0:T(8,128)(2,1)} %bitcast.30) | data formatting | bytes 1638400
  (3 shorter events, 0.0 us)

commit v2 on v1

v2 whole, which is shorter than its diff:
```python
import functools

import jax
import jax.numpy as jnp
import numpy as np
from jax import lax
from jax.experimental import pallas as pl
from jax.experimental.pallas import tpu as pltpu
from jax.sharding import PartitionSpec as P

KB = 128
MESH = pl.DeviceIdType.MESH
F32 = jnp.float32
BF16 = jnp.bfloat16
VMEM = pltpu.VMEM
MIB = 1024 * 1024
LIMIT = 24 * MIB


def spaces(*kinds):
    return [pl.BlockSpec(memory_space=k) for k in kinds]


def gate_rows(vox, table, w_gate, select, write, rows):
    lanes = lax.broadcasted_iota(jnp.int32, (256, KB), 1).astype(F32)
    for start in range(0, rows, 256):
        size = min(256, rows - start)
        logits = jnp.dot(vox(start, size), w_gate[...], preferred_element_type=F32)
        spread = lax.dot_general(
            table(start, size), select[...], (((0,), (0,)), ((), ())), preferred_element_type=F32
        )
        total = jnp.zeros((size, KB), F32)
        for p in range(4):
            gate = jax.nn.sigmoid(logits[:, p * KB : (p + 1) * KB])
            coef = (spread[:, (4 + p) * KB : (5 + p) * KB] * gate).astype(BF16).astype(F32)
            hit = spread[:, p * KB : (p + 1) * KB] == lanes[:size]
            total = total + jnp.where(hit, coef, 0.0)
        write(start, size, total.astype(BF16))


def collect(
    ns, nc, img, vox, coarse, table, base, w_point, select, w_up,
    feats, onehot, up, vox_halo, base_halo,
    coarse_halo, table_halo, dup, w_gate, local_sem,
    z_send, x_send, c_send, recv, c_recv, h_send, h_recv,
):
    clip, s, x, c = [lax.axis_index(a) for a in ("clip", "slab", "chan", "zs")]
    index = s * nc + x
    rows = vox.shape[1]

    def dev(s_, x_, c_):
        return (clip, s_, x_, c_)

    following, previous = index + 1, index - 1
    relations = [
        (s + 1 < ns, dev(s + 1, x, c)),
        (s > 0, dev(s - 1, x, c)),
        (x + 1 < nc, dev(s, x + 1, c)),
        (x > 0, dev(s, x - 1, c)),
        (following < ns * nc, dev(following // nc, following % nc, c)),
        (index > 0, dev(previous // nc, previous % nc, c)),
        (None, dev(s, x, 1 - c)),
    ]
    barrier = pltpu.get_barrier_semaphore()
    expected = 0
    for there, who in relations:
        def greet(who=who):
            pl.semaphore_signal(barrier, inc=1, device_id=who, device_id_type=MESH)
        if there is None:
            greet()
            expected = expected + 1
        else:
            pl.when(there)(greet)
            expected = expected + there.astype(jnp.int32)
    pl.semaphore_wait(barrier, expected)

    def remote(src, dst, ss, rs, who):
        return pltpu.make_async_remote_copy(
            src_ref=src, dst_ref=dst, send_sem=ss, recv_sem=rs, device_id=who, device_id_type=MESH
        )

    keep = pltpu.make_async_copy(img, feats.at[s, x], local_sem)
    keep.start()

    def part(s_, x_, q):
        return feats.at[s_, x_, c, q]

    sides = ((0, following < ns * nc, relations[4][1], 1), (1, index > 0, relations[5][1], 0))

    def halo_copies(side, who, row):
        pairs = (
            (table.at[row], table_halo.at[side]),
            (base.at[row], base_halo.at[side]),
            (coarse, coarse_halo.at[side]),
            (vox.at[row], vox_halo.at[side]),
        )
        return [
            remote(a, b, h_send.at[side, i], h_recv.at[side, i], who)
            for i, (a, b) in enumerate(pairs)
        ]

    def z_copy(si, xi, q, d, src=None):
        dst = part(si, xi, q)
        who = dev(s + 1 - 2 * d, x, c)
        return remote(dst if src is None else src, dst, z_send.at[d, q, si, xi], recv.at[q, si, xi], who)

    def x_copy(si, xi, q, d, src=None):
        dst = part(si, xi, q)
        who = dev(s, x + 1 - 2 * d, c)
        return remote(dst if src is None else src, dst, x_send.at[d, q, si, xi], recv.at[q, si, xi], who)

    def c_copy(si, xi, q):
        src = part(si, xi, q)
        return remote(src, src, c_send.at[q, si, xi], c_recv.at[q, si, xi], dev(s, x, 1 - c))

    z_ends = ((0, s + 1 < ns), (1, s > 0))
    x_ends = ((0, x + 1 < nc), (1, x > 0))

    def start_own(copy, ends, q):
        for d, there in ends:
            @pl.when(there)
            def _(d=d):
                copy(s, x, q, d, img.at[c, q]).start()

    start_own(x_copy, x_ends, 1)
    start_own(z_copy, z_ends, 0)
    start_own(z_copy, z_ends, 1)
    for side, there, who, row in sides:
        @pl.when(there)
        def _(side=side, who=who, row=row):
            for copy in halo_copies(side, who, row):
                copy.start()
    start_own(x_copy, x_ends, 0)

    def z_step(k, q):
        for xi in ((x,) if q == 0 else range(nc)):
            for d, si, there, on in (
                (0, s - k, s - k >= 0, s + 1 < ns),
                (1, s + k, s + k < ns, s > 0),
            ):
                @pl.when(there)
                def _(d=d, si=si, xi=xi, on=on):
                    z_copy(si, xi, q, d).wait_recv()

                    @pl.when(on)
                    def _():
                        z_copy(si, xi, q, d).start()

                    if q == 0:
                        for e, far in x_ends:
                            @pl.when(far)
                            def _(e=e):
                                x_copy(si, xi, q, e).start()
                    c_copy(si, xi, q).start()

    def x_step(k, q):
        items = ((s, True),) if k == 0 else ((s - k, s - k >= 0), (s + k, s + k < ns))
        for j in range(1, nc):
            for si, there_s in items:
                for d, xi, there_x, on in (
                    (0, x - j, x - j >= 0, x + 1 < nc),
                    (1, x + j, x + j < nc, x > 0),
                ):
                    @pl.when(jnp.logical_and(there_s, there_x))
                    def _(d=d, si=si, xi=xi, on=on):
                        x_copy(si, xi, q, d).wait_recv()
                        if nc > 2:
                            @pl.when(on)
                            def _():
                                x_copy(si, xi, q, d).start()
                        if q == 1:
                            for e, far in z_ends:
                                @pl.when(far)
                                def _(e=e):
                                    z_copy(si, xi, q, e).start()
                        c_copy(si, xi, q).start()

    def gates(row, vox_ref, table_ref, source):
        gate_rows(
            lambda a, n: vox_ref[source, a : a + n, :],
            lambda a, n: table_ref[source, :, a : a + n],
            w_gate, select,
            lambda a, n, v: onehot.__setitem__((row, slice(a, a + n)), v),
            rows,
        )

    def up_rows():
        count = coarse.shape[0]
        double = []
        for side in range(3):
            ref = coarse if side == 2 else coarse_halo.at[side]
            value = ref[...].astype(F32)
            dup[pl.ds(0, count, stride=2), :] = value
            dup[pl.ds(1, count, stride=2), :] = value
            value = dup[...]
            if side < 2:
                value = jnp.where((index > 0) if side == 0 else (following < ns * nc), value, 0.0)
            double.append(value.astype(BF16))
        even = lax.broadcasted_iota(jnp.int32, (2 * count, KB), 0) % 2 == 0
        gap = jnp.zeros((8, KB), F32)
        for px, (near, far, side) in enumerate(((1, 3, 0), (2, 0, 1))):
            lhs = jnp.concatenate([double[2], double[side]], axis=1)

            def tap(b):
                rhs = jnp.concatenate(
                    [jnp.concatenate([w_up[a, b, 0], w_up[a, b, 1]], axis=1) for a in (near, far)],
                    axis=0,
                )
                out = jnp.dot(lhs, rhs, preferred_element_type=F32)
                return jnp.where(even, out[:, :KB], out[:, KB:])

            first_y = tap(1) + jnp.concatenate([gap, tap(3)[:-8]], axis=0)
            up[px, :, 0] = first_y.reshape(-1, 8, KB)
            second_y = tap(2) + jnp.concatenate([tap(0)[8:], gap], axis=0)
            up[px, :, 1] = second_y.reshape(-1, 8, KB)

    w_gate[...] = jnp.dot(
        w_point[...].astype(F32), select[:4, : 4 * KB], preferred_element_type=F32
    ).astype(BF16)
    gates(1, vox, table, 0)
    x_step(0, 1)
    for k in range(1, ns):
        z_step(k, 0)
        z_step(k, 1)
        if k == 1:
            gates(2, vox, table, 1)
        x_step(k - 1, 0)
    for side, there, row in ((0, index > 0, 0), (1, following < ns * nc, 1)):
        @pl.when(there)
        def _(side=side, row=row):
            for copy in halo_copies(side, relations[4 + side][1], row):
                copy.wait_recv()

        @pl.when(jnp.logical_not(there))
        def _(side=side, row=row):
            table_halo[side] = table[row]
            base_halo[side] = base[row]
            coarse_halo[side] = coarse[...]
            vox_halo[side] = vox[row]
    up_rows()
    gates(0, vox_halo, table_halo, 0)
    gates(3, vox_halo, table_halo, 1)
    x_step(ns - 1, 0)

    for si in range(ns):
        for xi in range(nc):
            for q in range(2):
                @pl.when(jnp.logical_or(si != s, xi != x))
                def _(si=si, xi=xi, q=q):
                    dst = feats.at[si, xi, 1 - c, q]
                    sems = (c_send.at[q, si, xi], c_recv.at[q, si, xi])
                    remote(dst, dst, *sems, dev(s, x, 1 - c)).wait_recv()
                    c_copy(si, xi, q).wait_send()
    keep.wait()
    for side, there, who, row in sides:
        @pl.when(there)
        def _(side=side, who=who, row=row):
            for copy in halo_copies(side, who, row):
                copy.wait_send()
    for si in range(ns):
        for xi in range(nc):
            for d, there in z_ends:
                passed = (si <= s) if d == 0 else (si >= s)
                for q in range(2):
                    sent = jnp.logical_and(there, passed)
                    if q == 0:
                        sent = jnp.logical_and(sent, xi == x)

                    @pl.when(sent)
                    def _(d=d, si=si, xi=xi, q=q):
                        z_copy(si, xi, q, d).wait_send()
            for d, there in x_ends:
                passed = (xi <= x) if d == 0 else (xi >= x)
                for q in range(2):
                    sent = jnp.logical_and(there, passed)
                    if q == 1:
                        sent = jnp.logical_and(sent, si == s)

                    @pl.when(sent)
                    def _(d=d, si=si, xi=xi, q=q):
                        x_copy(si, xi, q, d).wait_send()


def attend(
    ns, nc, base, feats, onehot, vox, vox_halo, w_out, attended, face_in, sampled, face, wide, send, recv
):
    clip, s, x, c = [lax.axis_index(a) for a in ("clip", "slab", "chan", "zs")]
    index = s * nc + x
    other = (clip, s, x, 1 - c)
    rows = vox.shape[1]
    count = rows // 8
    barrier = pltpu.get_barrier_semaphore()
    pl.semaphore_signal(barrier, inc=1, device_id=other, device_id_type=MESH)
    pl.semaphore_wait(barrier, 1)

    def sample(r):
        def quad(i, carry):
            start = pl.multiple_of(i * 32, 32)
            lhs = onehot[r, pl.ds(start, 32), :]
            gap = jnp.zeros((16, KB), BF16)
            lhs = jnp.concatenate(
                [
                    jnp.concatenate([lhs[:16], gap], axis=1),
                    jnp.concatenate([gap, lhs[16:]], axis=1),
                ],
                axis=0,
            )
            block = [feats[base[r, 4 * i + j]] for j in range(4)]
            rhs = jnp.concatenate(
                [jnp.concatenate(block[:2], axis=1), jnp.concatenate(block[2:], axis=1)], axis=0
            )
            out = jnp.dot(lhs, rhs, preferred_element_type=F32)
            picked = jnp.concatenate(
                [out[:8, :KB], out[8:16, KB:], out[16:24, :KB], out[24:, KB:]], axis=0
            )
            sampled[pl.ds(start, 32), :] = picked.astype(BF16)
            return carry

        lax.fori_loop(0, rows // 32, quad, 0, unroll=5)

    copies = []
    for r in range(4):
        sample(r)
        mixed = jnp.dot(sampled[...], w_out[...], preferred_element_type=F32)
        query = vox[r - 1] if r in (1, 2) else vox_halo[r // 3]
        total = query.astype(F32) + mixed
        if r == 0:
            total = jnp.where(index > 0, total, 0.0)
        if r == 3:
            total = jnp.where(index < ns * nc - 1, total, 0.0)
        wide[...] = total
        attended[r] = total.astype(BF16)
        edge = jnp.where(c == 0, wide[pl.ds(7, count, stride=8), :], wide[pl.ds(0, count, stride=8), :])
        face[r, pl.ds(0, count), :] = edge.astype(BF16)
        copy = pltpu.make_async_remote_copy(
            src_ref=face.at[r], dst_ref=face_in.at[r], send_sem=send.at[r], recv_sem=recv.at[r],
            device_id=other, device_id_type=MESH,
        )
        copy.start()
        copies.append(copy)
    for copy in copies:
        copy.wait()


def convolve(attended, face_in, up, w_conv, out, wide, rhs, below, above, acc):
    c = lax.axis_index("zs")
    rows = attended.shape[1]
    count = rows // 8
    for a in range(3):
        for b in range(3):
            rhs[a * 3 * KB : (a + 1) * 3 * KB, b * KB : (b + 1) * KB] = w_conv[a, b]
    nothing = jnp.zeros((1, KB), F32)
    for r in range(4):
        value = attended[r].astype(F32)
        edge = face_in[r, pl.ds(0, count), :].astype(F32)
        below[...] = jnp.concatenate([nothing, value[:-1]], axis=0)
        below[pl.ds(0, count, stride=8), :] = jnp.where(c == 1, edge, 0.0)
        above[...] = jnp.concatenate([value[1:], nothing], axis=0)
        above[pl.ds(7, count, stride=8), :] = jnp.where(c == 0, edge, 0.0)
        wide[:, 3 * r * KB : (3 * r + 1) * KB] = below[...].astype(BF16)
        wide[:, (3 * r + 1) * KB : (3 * r + 2) * KB] = attended[r]
        wide[:, (3 * r + 2) * KB : (3 * r + 3) * KB] = above[...].astype(BF16)
    step = rows // 5
    for o in range(2):
        acc[...] = jnp.zeros_like(acc)

        def chunk(i, carry):
            start = pl.multiple_of(i * step, step)
            lhs = wide[pl.ds(start, step), 3 * o * KB : 3 * (o + 3) * KB]
            part = jnp.dot(lhs, rhs[...], preferred_element_type=F32)
            for b in range(3):
                acc[pl.ds(start + 16 - 8 * b, step), :] += part[:, b * KB : (b + 1) * KB]
            return carry

        lax.fori_loop(0, 5, chunk, 0)
        conv = jnp.maximum(acc[8 : 8 + rows, :], 0.0)
        total = attended[1 + o].astype(F32) + conv + up[o]
        out[o] = total.reshape(count, 8, KB).astype(BF16)


def body(
    voxels, image_feat, coarse, wedge_ids, hit_block, corners, bilinear, w_point, w_out, w_conv, w_up
):
    ns, nc = lax.axis_size("slab"), lax.axis_size("chan")
    rows_x, cols_y, layers, channels = voxels.shape
    rows = cols_y * layers
    pixels = image_feat.shape[0]
    quarter = pixels // 4
    blocks = pixels // KB
    vox = voxels.reshape(rows_x, rows, channels)
    small = coarse.reshape(-1, channels)
    both = jnp.concatenate([corners.astype(F32), bilinear.astype(F32)], axis=0)
    table = jnp.transpose(both.reshape(8, rows_x, rows), (1, 0, 2))
    base = wedge_ids[:, :, 0] * blocks + hit_block
    base = jnp.pad(base, ((0, 0), (0, 1024 - cols_y))).reshape(rows_x, 8, 128)
    select = np.repeat(np.eye(8, dtype=np.float32), KB, axis=1)
    dma = pltpu.SemaphoreType.DMA
    feats, onehot, up, vox_halo, base_halo = pl.pallas_call(
        functools.partial(collect, ns, nc),
        name="collect",
        out_shape=(
            jax.ShapeDtypeStruct((ns, nc, 2, 2, quarter, channels), BF16),
            jax.ShapeDtypeStruct((4, rows, KB), BF16),
            jax.ShapeDtypeStruct((2, cols_y // 2, 2, layers, channels), F32),
            jax.ShapeDtypeStruct((2, rows, channels), BF16),
            jax.ShapeDtypeStruct((2, 8, 128), jnp.int32),
        ),
        in_specs=spaces(pl.ANY, *[VMEM] * 7),
        out_specs=tuple(spaces(pl.ANY, *[VMEM] * 4)),
        scratch_shapes=[
            VMEM((2,) + small.shape, BF16),
            VMEM((2, 8, rows), F32),
            VMEM((2 * small.shape[0], channels), F32),
            VMEM((channels, 4 * KB), BF16),
            dma(()),
            dma((2, 2, ns, nc)),
            dma((2, 2, ns, nc)),
            dma((2, ns, nc)),
            dma((2, ns, nc)),
            dma((2, ns, nc)),
            dma((2, 4)),
            dma((2, 4)),
        ],
        compiler_params=pltpu.CompilerParams(
            collective_id=0, has_side_effects=True, vmem_limit_bytes=LIMIT
        ),
    )(image_feat.reshape(2, 2, quarter, channels), vox, small, table, base, w_point, select, w_up)
    index = jnp.concatenate([base_halo[:1], base, base_halo[1:]], axis=0).reshape(4, 1024)
    blocks_all = feats.reshape(ns * nc * blocks, KB, channels)
    attended, face_in = pl.pallas_call(
        functools.partial(attend, ns, nc),
        name="attend",
        out_shape=(
            jax.ShapeDtypeStruct((4, rows, channels), BF16),
            jax.ShapeDtypeStruct((4, 208, channels), BF16),
        ),
        in_specs=spaces(pltpu.SMEM, *[VMEM] * 5),
        out_specs=tuple(spaces(VMEM, VMEM)),
        scratch_shapes=[
            VMEM((rows, channels), BF16),
            VMEM((4, 208, channels), BF16),
            VMEM((rows, channels), F32),
            dma((4,)),
            dma((4,)),
        ],
        compiler_params=pltpu.CompilerParams(
            collective_id=1, has_side_effects=True, vmem_limit_bytes=16 * MIB + 2 * blocks_all.size
        ),
    )(index, blocks_all, onehot, vox, vox_halo, w_out)
    return pl.pallas_call(
        convolve,
        name="convolve",
        out_shape=jax.ShapeDtypeStruct(voxels.shape, BF16),
        in_specs=spaces(*[VMEM] * 4),
        out_specs=pl.BlockSpec(memory_space=VMEM),
        scratch_shapes=[
            VMEM((rows, 12 * KB), BF16),
            VMEM((9 * KB, 3 * KB), BF16),
            VMEM((rows, KB), F32),
            VMEM((rows, KB), F32),
            VMEM((rows + 16, KB), F32),
        ],
        compiler_params=pltpu.CompilerParams(vmem_limit_bytes=24 * MIB),
    )(attended, face_in, up.reshape(2, rows, channels), w_conv.reshape(3, 3, 3 * channels, channels))


def solution(mesh):
    return jax.shard_map(
        body,
        mesh=mesh,
        in_specs=(
            P(("clip", "slab", "chan"), None, "zs", None),
            P(("clip", "slab", "chan"), None),
            P(("clip", "slab", "chan"), None, "zs", None),
            P(("clip", "slab", "chan"), None, None),
            P(("clip", "slab", "chan"), None),
            P("clip", ("slab", "chan"), None, "zs"),
            P("clip", ("slab", "chan"), None, "zs"),
            P(),
            P(),
            P(),
            P(),
        ),
        out_specs=P(("clip", "slab", "chan"), None, "zs", None),
        check_vma=False,
    )
```

time: 96.6 us -> 80.5 us (0.83)
  the two profiles are of different devices: /device:TPU:17 before, /device:TPU:0 now
where the time goes in v2:
time: 80.5 us; the launch traced here: 80.2 us
  Pallas kernels  73.2 us (91%)
  local copies, waits for them, and re-layouts  4.47 us (6%)
  other arithmetic  2.34 us (3%)
    pallas_call x1, Pallas kernels, body(): pl.pallas_call(functools.partial(collect, ns, nc), name='collect', out_sh...  51.4 us
    pallas_call x1, Pallas kernels, body(): pl.pallas_call(functools.partial(attend, ns, nc), name='attend', out_shap...  12.9 us
    pallas_call x1, Pallas kernels, body(): pl.pallas_call(convolve, name='convolve', out_shape=jax.ShapeDtypeStruct(...  8.91 us
    reshape x1, local copies, waits for them, and re-layouts, body(): table = jnp.transpose(both.reshape(8, rows_x, rows), (1, 0, 2))  1.9 us
    concatenate x1, local copies, waits for them, and re-layouts, body(): both = jnp.concatenate([corners.astype(F32), bilinear.astype(F32)], axis=0)  1.7 us
    convert_element_type x2, other arithmetic, body(): both = jnp.concatenate([corners.astype(F32), bilinear.astype(F32)], axis=0)  1.61 us

profile of v2, /device:TPU:0, one launch (start us, length us, event | category | flops | bytes accessed | tf_op | source)
XLA Modules:
  0.0 80.2 jit_solution(10041279441899515275)
XLA Ops:
  0.0 0.7 bitcast_add_fusion
  0.7 0.8 %copy.18.w_point = bf16[128,4]{1,0:T(8,128)(2,1)S(1)} copy(bf16[128,4]{0,1:T(4,128)(2,1)} %param.19) | data formatting | bytes 2048 | tf_op args[7]
  1.5 0.8 %convert_element_type.6 = f32[4,2,200,8]{2,3,1,0:T(8,128)S(1)} convert(s32[4,2,200,8]{2,3,1,0:T(8,128)} %param.17) | non-fusion elementwise | flops 12800 | bytes 102400 | tf_op jit(solution)/shard_map/convert_element_type | solution.py:392
  2.4 0.8 convert_element_type.7
  3.2 0.0 copy-start
  3.2 0.0 copy-start.1
  3.2 0.0 copy-start.3
  3.2 0.0 copy-start.4
  3.2 0.0 copy-start.6
  3.2 1.7 %copy.16 = f32[8,2,200,8]{3,2,0,1:T(8,128)} copy(f32[8,2,200,8]{2,3,1,0:T(8,128)S(1)} %pad_maximum_fusion) | data formatting | bytes 204800 | tf_op jit(solution)/shard_map/concatenate | solution.py:392
  4.9 1.9 %reshape.34 = f32[8,2,1600]{2,0,1:T(8,128)S(1)} reshape(f32[8,2,200,8]{3,2,0,1:T(8,128)} %copy.16) | data formatting | bytes 204800 | tf_op jit(solution)/shard_map/reshape | solution.py:393
  6.8 0.0 copy-start.5
  6.8 0.0 copy-done
  6.8 0.0 copy-done.1
  6.9 0.0 copy-done.3
  6.9 0.0 copy-done.4
  6.9 0.0 copy-done.6
  6.9 51.4 %collect.1 = (bf16[4,2,2,2,512,128]{5,4,3,2,1,0:T(8,128)(2,1)S(1)}, bf16[4,1600,128]{2,1,0:T(8,128)(2,1)S(1)}, f32[2,100,2,8,128]{4,3,2,1,0:T(8,128)S(1)}, bf16[...) custom-call(bf16[2,2,512,128]{3,2,1,0:T(8,128)(2,1)S(1)} %bitcast.25, bf16[2,1600,128]{2,1,0:T(8,128)(2,1)S(1)} %bitcast.21, ...), custom_call_target="tpu_custom_call" | custom-call | tf_op jit(solution)/shard_map/collect/pallas_call | solution.py:398
  58.4 0.0 copy-done.5
  58.4 0.0 copy-start.2
  58.4 12.9 %attend.1 = (bf16[4,1600,128]{2,1,0:T(8,128)(2,1)S(1)}, bf16[4,208,128]{2,1,0:T(8,128)(2,1)S(1)}) custom-call(s32[4,1024]{1,0:T(4,128)S(1)} %pad_add_fusion.base, bf16[128,128,128]{2,1,0:T(8,128)(2,1)S(1)} %bitcast.20, bf16[4,1600,128]{2,1,0:T(8,128)(2,1)S(1)} %get-tuple-element.14.onehot, bf16[2,1600,128]{2,1,0:T(8,128)(2,1)S(1)} %bitcast.22, ...), custom_call_target="tpu_custom_call" | custom-call | tf_op jit(solution)/shard_map/attend/pallas_call | solution.py:430
  71.3 0.0 copy-done.2
  71.3 8.9 %convolve.1 = bf16[2,200,8,128]{3,2,1,0:T(8,128)(2,1)} custom-call(bf16[4,1600,128]{2,1,0:T(8,128)(2,1)S(1)} %get-tuple-element.16.attended, bf16[4,208,128]{2,1,0:T(8,128)(2,1)S(1)} %get-tuple-element.17.face_in, f32[2,1600,128]{2,1,0:T(8,128)S(1)} %bitcast.23, bf16[3,3,384,128]{3,2,1,0:T(8,128)(2,1)S(1)} %bitcast.24), custom_call_target="tpu_custom_call" | custom-call | tf_op jit(solution)/shard_map/convolve/pallas_call | solution.py:450
  (5 shorter events, 0.0 us)
Async XLA Ops:
  3.2 3.7 %copy-start = (bf16[2,200,8,128]{3,2,1,0:T(8,128)(2,1)S(1)}, bf16[2,200,8,128]{3,2,1,0:T(8,128)(2,1)}, u32[]{:S(2)}) copy-start(bf16[2,200,8,128]{3,2,1,0:T(8,128)(2,1)} %param.12) | copy-start | bytes 2457604
  3.2 3.7 %copy-start.1 = (bf16[4,4,2,128,128]{4,3,2,1,0:T(8,128)(2,1)S(1)}, bf16[4,4,2,128,128]{4,3,2,1,0:T(8,128)(2,1)}, u32[]{:S(2)}) copy-start(bf16[4,4,2,128,128]{4,3,2,1,0:T(8,128)(2,1)} %w_up.1) | copy-start | bytes 3145732
  3.2 3.7 %copy-start.3 = (bf16[2048,128]{1,0:T(8,128)(2,1)S(1)}, bf16[2048,128]{1,0:T(8,128)(2,1)}, u32[]{:S(2)}) copy-start(bf16[2048,128]{1,0:T(8,128)(2,1)} %param.13) | copy-start | bytes 1572868
  3.2 3.7 %copy-start.4 = (bf16[1,100,4,128]{3,2,1,0:T(4,128)(2,1)S(1)}, bf16[1,100,4,128]{3,2,1,0:T(4,128)(2,1)}, u32[]{:S(2)}) copy-start(bf16[1,100,4,128]{3,2,1,0:T(4,128)(2,1)} %param.14) | copy-start | bytes 307204
  3.2 3.7 %copy-start.6 = (f32[8,1024]{1,0:T(8,128)S(1)}, f32[8,1024]{1,0:T(8,128)}, u32[]{:S(2)}) copy-start(f32[8,1024]{1,0:T(8,128)} %constant.6.clone.select) | copy-start | bytes 98308
  6.8 51.5 %copy-start.5 = (bf16[128,128]{1,0:T(8,128)(2,1)S(1)}, bf16[128,128]{1,0:T(8,128)(2,1)}, u32[]{:S(2)}) copy-start(bf16[128,128]{1,0:T(8,128)(2,1)} %w_out.1) | copy-start | bytes 98308
  58.4 12.9 %copy-start.2 = (bf16[3,3,3,128,128]{4,3,2,1,0:T(8,128)(2,1)S(1)}, bf16[3,3,3,128,128]{4,3,2,1,0:T(8,128)(2,1)}, u32[]{:S(2)}) copy-start(bf16[3,3,3,128,128]{4,3,2,1,0:T(8,128)(2,1)} %param.21) | copy-start | bytes 2654212

commit v3 on v2

--- a/solution.py
+++ b/solution.py
@@ -2,7 +2,6 @@
 
 import jax
 import jax.numpy as jnp
-import numpy as np
 from jax import lax
 from jax.experimental import pallas as pl
 from jax.experimental.pallas import tpu as pltpu
@@ -21,32 +20,41 @@
     return [pl.BlockSpec(memory_space=k) for k in kinds]
 
 
-def gate_rows(vox, table, w_gate, select, write, rows):
-    lanes = lax.broadcasted_iota(jnp.int32, (256, KB), 1).astype(F32)
-    for start in range(0, rows, 256):
-        size = min(256, rows - start)
-        logits = jnp.dot(vox(start, size), w_gate[...], preferred_element_type=F32)
-        spread = lax.dot_general(
-            table(start, size), select[...], (((0,), (0,)), ((), ())), preferred_element_type=F32
-        )
-        total = jnp.zeros((size, KB), F32)
+def gate_rows(vox, table, w_gate, query, hits):
+    query[...] = vox.astype(F32)
+    count = query.shape[0] // 8
+    lanes = lax.broadcasted_iota(jnp.int32, (count, KB), 1).astype(F32)
+    entry = lax.broadcasted_iota(jnp.int32, (64, 8 * KB), 0)
+    wanted = lax.broadcasted_iota(jnp.int32, (64, 8 * KB), 1) // KB * 8
+    values = table.reshape(64, -1).T[:count]
+    for z in range(8):
+        of_layer = pl.ds(z, count, stride=8)
+        logits = jnp.dot(query[of_layer, :].astype(BF16), w_gate[...], preferred_element_type=F32)
+        select = jnp.where(entry == wanted + z, 1.0, 0.0)
+        spread = jnp.dot(values, select, preferred_element_type=F32)
+        total = jnp.zeros((count, KB), F32)
         for p in range(4):
             gate = jax.nn.sigmoid(logits[:, p * KB : (p + 1) * KB])
             coef = (spread[:, (4 + p) * KB : (5 + p) * KB] * gate).astype(BF16).astype(F32)
-            hit = spread[:, p * KB : (p + 1) * KB] == lanes[:size]
+            hit = spread[:, p * KB : (p + 1) * KB] == lanes
             total = total + jnp.where(hit, coef, 0.0)
-        write(start, size, total.astype(BF16))
+        hits[of_layer, :] = total
+    return hits[...].astype(BF16)
 
 
 def collect(
-    ns, nc, img, vox, coarse, table, base, w_point, select, w_up,
+    ns, nc, img, vox, coarse, corners, bilinear, base, w_point, w_up,
     feats, onehot, up, vox_halo, base_halo,
-    coarse_halo, table_halo, dup, w_gate, local_sem,
+    coarse_halo, table, table_halo, dup, w_gate, query, hits, local_sem,
     z_send, x_send, c_send, recv, c_recv, h_send, h_recv,
 ):
     clip, s, x, c = [lax.axis_index(a) for a in ("clip", "slab", "chan", "zs")]
     index = s * nc + x
-    rows = vox.shape[1]
+    columns = corners.shape[3]
+    for row in range(2):
+        for p in range(4):
+            table[row, p, :, :columns] = corners[p, row].astype(F32)
+            table[row, 4 + p, :, :columns] = bilinear[p, row].astype(F32)
 
     def dev(s_, x_, c_):
         return (clip, s_, x_, c_)
@@ -176,13 +184,7 @@
                         c_copy(si, xi, q).start()
 
     def gates(row, vox_ref, table_ref, source):
-        gate_rows(
-            lambda a, n: vox_ref[source, a : a + n, :],
-            lambda a, n: table_ref[source, :, a : a + n],
-            w_gate, select,
-            lambda a, n, v: onehot.__setitem__((row, slice(a, a + n)), v),
-            rows,
-        )
+        onehot[row] = gate_rows(vox_ref[source], table_ref[source], w_gate, query, hits)
 
     def up_rows():
         count = coarse.shape[0]
@@ -214,17 +216,19 @@
             second_y = tap(2) + jnp.concatenate([tap(0)[8:], gap], axis=0)
             up[px, :, 1] = second_y.reshape(-1, 8, KB)
 
-    w_gate[...] = jnp.dot(
-        w_point[...].astype(F32), select[:4, : 4 * KB], preferred_element_type=F32
+    point = lax.broadcasted_iota(jnp.int32, (4, 4 * KB), 0)
+    spread = jnp.where(point == lax.broadcasted_iota(jnp.int32, (4, 4 * KB), 1) // KB, 1.0, 0.0)
+    w_gate[...] = lax.dot_general(
+        w_point[...].astype(F32), spread, (((0,), (0,)), ((), ())), preferred_element_type=F32
     ).astype(BF16)
-    gates(1, vox, table, 0)
     x_step(0, 1)
     for k in range(1, ns):
         z_step(k, 0)
         z_step(k, 1)
         if k == 1:
+            gates(1, vox, table, 0)
+        if k == 2:
             gates(2, vox, table, 1)
-        x_step(k - 1, 0)
     for side, there, row in ((0, index > 0, 0), (1, following < ns * nc, 1)):
         @pl.when(there)
         def _(side=side, row=row):
@@ -240,7 +244,8 @@
     up_rows()
     gates(0, vox_halo, table_halo, 0)
     gates(3, vox_halo, table_halo, 1)
-    x_step(ns - 1, 0)
+    for k in range(ns):
+        x_step(k, 0)
 
     for si in range(ns):
         for xi in range(nc):
@@ -316,7 +321,7 @@
             sampled[pl.ds(start, 32), :] = picked.astype(BF16)
             return carry
 
-        lax.fori_loop(0, rows // 32, quad, 0, unroll=5)
+        lax.fori_loop(0, rows // 32, quad, 0, unroll=25)
 
     copies = []
     for r in range(4):
@@ -360,7 +365,7 @@
         wide[:, 3 * r * KB : (3 * r + 1) * KB] = below[...].astype(BF16)
         wide[:, (3 * r + 1) * KB : (3 * r + 2) * KB] = attended[r]
         wide[:, (3 * r + 2) * KB : (3 * r + 3) * KB] = above[...].astype(BF16)
-    step = rows // 5
+    step = rows // 2
     for o in range(2):
         acc[...] = jnp.zeros_like(acc)
 
@@ -372,7 +377,7 @@
                 acc[pl.ds(start + 16 - 8 * b, step), :] += part[:, b * KB : (b + 1) * KB]
             return carry
 
-        lax.fori_loop(0, 5, chunk, 0)
+        lax.fori_loop(0, 2, chunk, 0)
         conv = jnp.maximum(acc[8 : 8 + rows, :], 0.0)
         total = attended[1 + o].astype(F32) + conv + up[o]
         out[o] = total.reshape(count, 8, KB).astype(BF16)
@@ -389,11 +394,8 @@
     blocks = pixels // KB
     vox = voxels.reshape(rows_x, rows, channels)
     small = coarse.reshape(-1, channels)
-    both = jnp.concatenate([corners.astype(F32), bilinear.astype(F32)], axis=0)
-    table = jnp.transpose(both.reshape(8, rows_x, rows), (1, 0, 2))
     base = wedge_ids[:, :, 0] * blocks + hit_block
     base = jnp.pad(base, ((0, 0), (0, 1024 - cols_y))).reshape(rows_x, 8, 128)
-    select = np.repeat(np.eye(8, dtype=np.float32), KB, axis=1)
     dma = pltpu.SemaphoreType.DMA
     feats, onehot, up, vox_halo, base_halo = pl.pallas_call(
         functools.partial(collect, ns, nc),
@@ -409,9 +411,12 @@
         out_specs=tuple(spaces(pl.ANY, *[VMEM] * 4)),
         scratch_shapes=[
             VMEM((2,) + small.shape, BF16),
-            VMEM((2, 8, rows), F32),
+            VMEM((2, 8, layers, 256), F32),
+            VMEM((2, 8, layers, 256), F32),
             VMEM((2 * small.shape[0], channels), F32),
             VMEM((channels, 4 * KB), BF16),
+            VMEM((rows, channels), F32),
+            VMEM((rows, KB), F32),
             dma(()),
             dma((2, 2, ns, nc)),
             dma((2, 2, ns, nc)),
@@ -424,7 +429,8 @@
         compiler_params=pltpu.CompilerParams(
             collective_id=0, has_side_effects=True, vmem_limit_bytes=LIMIT
         ),
-    )(image_feat.reshape(2, 2, quarter, channels), vox, small, table, base, w_point, select, w_up)
+    )(image_feat.reshape(2, 2, quarter, channels), vox, small,
+      jnp.swapaxes(corners, 2, 3), jnp.swapaxes(bilinear, 2, 3), base, w_point.T, w_up)
     index = jnp.concatenate([base_halo[:1], base, base_halo[1:]], axis=0).reshape(4, 1024)
     blocks_all = feats.reshape(ns * nc * blocks, KB, channels)
     attended, face_in = pl.pallas_call(

time: 80.5 us -> 74.2 us (0.922)
  Pallas kernels: 73.2 us -> 66.4 us
  local copies, waits for them, and re-layouts: 4.47 us -> 6.6 us
  other arithmetic: 2.34 us -> 0.72 us
    unnamed x16 -> x21, local copies, waits for them, and re-layouts: 0.86 us -> 6.59 us
    pallas_call x1, Pallas kernels: 12.9 us -> 8.61 us  [body(): pl.pallas_call(functools.partial(attend, ns, nc), name='attend', out_shap...]
    reshape x1 -> x0, local copies, waits for them, and re-layouts: 1.9 us -> none  [body(): table = jnp.transpose(both.reshape(8, rows_x, rows), (1, 0, 2))]
    concatenate x1 -> x0, local copies, waits for them, and re-layouts: 1.7 us -> none  [body(): both = jnp.concatenate([corners.astype(F32), bilinear.astype(F32)], axis=0)]
    convert_element_type x2 -> x0, other arithmetic: 1.61 us -> none  [body(): both = jnp.concatenate([corners.astype(F32), bilinear.astype(F32)], axis=0)]
    pallas_call x1, Pallas kernels: 51.4 us -> 50.1 us  [body(): pl.pallas_call(functools.partial(collect, ns, nc), name='collect', out_sh...]
    pallas_call x1, Pallas kernels: 8.91 us -> 7.63 us  [body(): pl.pallas_call(convolve, name='convolve', out_shape=jax.ShapeDtypeStruct(...]
where the time goes in v3:
time: 74.2 us; the launch traced here: 73.8 us
  Pallas kernels  66.4 us (89%)
  local copies, waits for them, and re-layouts  6.6 us (9%)
    pallas_call x1, Pallas kernels, body(): pl.pallas_call(functools.partial(collect, ns, nc), name='collect', out_sh...  50.1 us
    pallas_call x1, Pallas kernels, body(): pl.pallas_call(functools.partial(attend, ns, nc), name='attend', out_shap...  8.61 us
    pallas_call x1, Pallas kernels, body(): pl.pallas_call(convolve, name='convolve', out_shape=jax.ShapeDtypeStruct(...  7.63 us
    unnamed x21, local copies, waits for them, and re-layouts  6.59 us

profile of v3, /device:TPU:0, one launch (start us, length us, event | category | flops | bytes accessed | tf_op | source)
XLA Modules:
  0.0 73.8 jit_solution(13365076494283017397)
XLA Ops:
  0.0 0.0 copy-start.8
  0.0 0.7 bitcast_add_fusion
  0.7 0.0 copy-start
  0.7 1.1 %copy-done = bf16[2,200,8,128]{3,2,1,0:T(8,128)(2,1)S(1)} copy-done((bf16[2,200,8,128]{3,2,1,0:T(8,128)(2,1)S(1)}, bf16[2,200,8,128]{3,2,1,0:T(8,128)(2,1)}, u32[]{:S(2)}) %copy-start) | copy-done | bytes 819224
  1.9 0.0 copy-start.2
  1.9 1.2 %copy-done.2 = bf16[4,4,2,128,128]{4,3,2,1,0:T(8,128)(2,1)S(1)} copy-done((bf16[4,4,2,128,128]{4,3,2,1,0:T(8,128)(2,1)S(1)}, bf16[4,4,2,128,128]{4,3,2,1,0:T(8,128)(2,1)}, u32[]{:S(2)}) %copy-start.2) | copy-done | bytes 1048600
  3.1 0.0 copy-start.4
  3.1 1.0 %copy-done.4 = bf16[2048,128]{1,0:T(8,128)(2,1)S(1)} copy-done((bf16[2048,128]{1,0:T(8,128)(2,1)S(1)}, bf16[2048,128]{1,0:T(8,128)(2,1)}, u32[]{:S(2)}) %copy-start.4) | copy-done | bytes 524312
  4.1 0.0 copy-start.5
  4.1 0.9 %copy-done.5 = bf16[1,100,4,128]{3,2,1,0:T(4,128)(2,1)S(1)} copy-done((bf16[1,100,4,128]{3,2,1,0:T(4,128)(2,1)S(1)}, bf16[1,100,4,128]{3,2,1,0:T(4,128)(2,1)}, u32[]{:S(2)}) %copy-start.5) | copy-done | bytes 102424
  5.0 0.0 copy-start.6
  5.0 0.8 %copy-done.6 = s32[4,2,200,8]{2,3,1,0:T(8,128)S(1)} copy-done((s32[4,2,200,8]{2,3,1,0:T(8,128)S(1)}, s32[4,2,200,8]{2,3,1,0:T(8,128)}, u32[]{:S(2)}) %copy-start.6) | copy-done | bytes 51224
  5.9 0.0 copy-start.7
  5.9 0.8 %copy-done.7 = bf16[4,2,200,8]{2,3,1,0:T(8,128)(2,1)S(1)} copy-done((bf16[4,2,200,8]{2,3,1,0:T(8,128)(2,1)S(1)}, bf16[4,2,200,8]{2,3,1,0:T(8,128)(2,1)}, u32[]{:S(2)}) %copy-start.7) | copy-done | bytes 25624
  6.6 0.0 copy-start.9
  6.6 0.7 copy-done.9
  7.3 0.0 copy-start.1
  7.3 50.1 %collect.1 = (bf16[4,2,2,2,512,128]{5,4,3,2,1,0:T(8,128)(2,1)S(1)}, bf16[4,1600,128]{2,1,0:T(8,128)(2,1)S(1)}, f32[2,100,2,8,128]{4,3,2,1,0:T(8,128)S(1)}, bf16[...) custom-call(bf16[2,2,512,128]{3,2,1,0:T(8,128)(2,1)S(1)} %bitcast.23, bf16[2,1600,128]{2,1,0:T(8,128)(2,1)S(1)} %bitcast.19, ...), custom_call_target="tpu_custom_call" | custom-call | tf_op jit(solution)/shard_map/collect/pallas_call | solution.py:400
  57.5 0.0 copy-done.8
  57.5 0.0 copy-done.1
  57.5 0.0 copy-start.3
  57.5 8.6 %attend.1 = (bf16[4,1600,128]{2,1,0:T(8,128)(2,1)S(1)}, bf16[4,208,128]{2,1,0:T(8,128)(2,1)S(1)}) custom-call(s32[4,1024]{1,0:T(4,128)S(1)} %pad_add_fusion.base, bf16[128,128,128]{2,1,0:T(8,128)(2,1)S(1)} %bitcast.18, bf16[4,1600,128]{2,1,0:T(8,128)(2,1)S(1)} %get-tuple-element.14.onehot, bf16[2,1600,128]{2,1,0:T(8,128)(2,1)S(1)} %bitcast.20, ...), custom_call_target="tpu_custom_call" | custom-call | tf_op jit(solution)/shard_map/attend/pallas_call | solution.py:436
  66.1 0.0 copy-done.3
  66.1 7.6 %convolve.1 = bf16[2,200,8,128]{3,2,1,0:T(8,128)(2,1)} custom-call(bf16[4,1600,128]{2,1,0:T(8,128)(2,1)S(1)} %get-tuple-element.16.attended, bf16[4,208,128]{2,1,0:T(8,128)(2,1)S(1)} %get-tuple-element.17.face_in, f32[2,1600,128]{2,1,0:T(8,128)S(1)} %bitcast.21, bf16[3,3,384,128]{3,2,1,0:T(8,128)(2,1)S(1)} %bitcast.22), custom_call_target="tpu_custom_call" | custom-call | tf_op jit(solution)/shard_map/convolve/pallas_call | solution.py:456
  (4 shorter events, 0.0 us)
Async XLA Ops:
  0.0 57.5 %copy-start.8 = (bf16[128,128]{1,0:T(8,128)(2,1)S(1)}, bf16[128,128]{1,0:T(8,128)(2,1)}, u32[]{:S(2)}) copy-start(bf16[128,128]{1,0:T(8,128)(2,1)} %w_out.1) | copy-start | bytes 98308
  0.7 1.1 %copy-start = (bf16[2,200,8,128]{3,2,1,0:T(8,128)(2,1)S(1)}, bf16[2,200,8,128]{3,2,1,0:T(8,128)(2,1)}, u32[]{:S(2)}) copy-start(bf16[2,200,8,128]{3,2,1,0:T(8,128)(2,1)} %param.11) | copy-start | bytes 2457604
  1.9 1.2 %copy-start.2 = (bf16[4,4,2,128,128]{4,3,2,1,0:T(8,128)(2,1)S(1)}, bf16[4,4,2,128,128]{4,3,2,1,0:T(8,128)(2,1)}, u32[]{:S(2)}) copy-start(bf16[4,4,2,128,128]{4,3,2,1,0:T(8,128)(2,1)} %w_up.1) | copy-start | bytes 3145732
  3.1 1.0 %copy-start.4 = (bf16[2048,128]{1,0:T(8,128)(2,1)S(1)}, bf16[2048,128]{1,0:T(8,128)(2,1)}, u32[]{:S(2)}) copy-start(bf16[2048,128]{1,0:T(8,128)(2,1)} %param.12) | copy-start | bytes 1572868
  4.1 0.9 %copy-start.5 = (bf16[1,100,4,128]{3,2,1,0:T(4,128)(2,1)S(1)}, bf16[1,100,4,128]{3,2,1,0:T(4,128)(2,1)}, u32[]{:S(2)}) copy-start(bf16[1,100,4,128]{3,2,1,0:T(4,128)(2,1)} %param.13) | copy-start | bytes 307204
  5.0 0.8 %copy-start.6 = (s32[4,2,200,8]{2,3,1,0:T(8,128)S(1)}, s32[4,2,200,8]{2,3,1,0:T(8,128)}, u32[]{:S(2)}) copy-start(s32[4,2,200,8]{2,3,1,0:T(8,128)} %param.16) | copy-start | bytes 153604
  5.9 0.8 %copy-start.7 = (bf16[4,2,200,8]{2,3,1,0:T(8,128)(2,1)S(1)}, bf16[4,2,200,8]{2,3,1,0:T(8,128)(2,1)}, u32[]{:S(2)}) copy-start(bf16[4,2,200,8]{2,3,1,0:T(8,128)(2,1)} %param.17) | copy-start | bytes 76804
  6.6 0.7 copy-start.9
  7.3 50.2 %copy-start.1 = (bf16[2,200,8,128]{3,2,1,0:T(8,128)(2,1)S(1)}, bf16[2,200,8,128]{3,2,1,0:T(8,128)(2,1)}, u32[]{:S(2)}) copy-start(bf16[2,200,8,128]{3,2,1,0:T(8,128)(2,1)} %param.11) | copy-start | bytes 2457604
  57.5 8.6 %copy-start.3 = (bf16[3,3,3,128,128]{4,3,2,1,0:T(8,128)(2,1)S(1)}, bf16[3,3,3,128,128]{4,3,2,1,0:T(8,128)(2,1)}, u32[]{:S(2)}) copy-start(bf16[3,3,3,128,128]{4,3,2,1,0:T(8,128)(2,1)} %param.20) | copy-start | bytes 2654212

commit v4 on v3

--- a/solution.py
+++ b/solution.py
@@ -26,11 +26,11 @@
     lanes = lax.broadcasted_iota(jnp.int32, (count, KB), 1).astype(F32)
     entry = lax.broadcasted_iota(jnp.int32, (64, 8 * KB), 0)
     wanted = lax.broadcasted_iota(jnp.int32, (64, 8 * KB), 1) // KB * 8
-    values = table.reshape(64, -1).T[:count]
+    values = table.astype(F32).T[:count].astype(BF16)
     for z in range(8):
         of_layer = pl.ds(z, count, stride=8)
         logits = jnp.dot(query[of_layer, :].astype(BF16), w_gate[...], preferred_element_type=F32)
-        select = jnp.where(entry == wanted + z, 1.0, 0.0)
+        select = jnp.where(entry == wanted + z, 1.0, 0.0).astype(BF16)
         spread = jnp.dot(values, select, preferred_element_type=F32)
         total = jnp.zeros((count, KB), F32)
         for p in range(4):
@@ -43,18 +43,25 @@
 
 
 def collect(
-    ns, nc, img, vox, coarse, corners, bilinear, base, w_point, w_up,
-    feats, onehot, up, vox_halo, base_halo,
-    coarse_halo, table, table_halo, dup, w_gate, query, hits, local_sem,
+    ns, nc, img, vox_hbm, coarse_hbm, corners_hbm, bilinear_hbm, wedge_hbm, hit_hbm, point_hbm, up_hbm,
+    feats, onehot, up, vox_halo, base,
+    vox, coarse, corners, bilinear, wedge, hit, w_point, w_up,
+    coarse_halo, table, table_halo, dup, w_gate, query, hits, local_sem, in_sem,
     z_send, x_send, c_send, recv, c_recv, h_send, h_recv,
 ):
     clip, s, x, c = [lax.axis_index(a) for a in ("clip", "slab", "chan", "zs")]
     index = s * nc + x
-    columns = corners.shape[3]
-    for row in range(2):
-        for p in range(4):
-            table[row, p, :, :columns] = corners[p, row].astype(F32)
-            table[row, 4 + p, :, :columns] = bilinear[p, row].astype(F32)
+    inputs = [
+        pltpu.make_async_copy(src, dst, in_sem.at[i])
+        for i, (src, dst) in enumerate(
+            (
+                (corners_hbm, corners), (bilinear_hbm, bilinear), (wedge_hbm, wedge), (hit_hbm, hit),
+                (point_hbm, w_point), (vox_hbm, vox), (coarse_hbm, coarse), (up_hbm, w_up),
+            )
+        )
+    ]
+    for copy in inputs:
+        copy.start()
 
     def dev(s_, x_, c_):
         return (clip, s_, x_, c_)
@@ -97,10 +104,10 @@
 
     def halo_copies(side, who, row):
         pairs = (
+            (coarse_hbm, coarse_halo.at[side]),
+            (vox_hbm.at[row], vox_halo.at[side]),
             (table.at[row], table_halo.at[side]),
-            (base.at[row], base_halo.at[side]),
-            (coarse, coarse_halo.at[side]),
-            (vox.at[row], vox_halo.at[side]),
+            (base.at[1 + row], base.at[3 * side]),
         )
         return [
             remote(a, b, h_send.at[side, i], h_recv.at[side, i], who)
@@ -136,9 +143,25 @@
     for side, there, who, row in sides:
         @pl.when(there)
         def _(side=side, who=who, row=row):
-            for copy in halo_copies(side, who, row):
+            for copy in halo_copies(side, who, row)[:2]:
                 copy.start()
     start_own(x_copy, x_ends, 0)
+    for copy in inputs:
+        copy.wait()
+    columns = corners.shape[3]
+    blocks = img.shape[0] * img.shape[1] * img.shape[2] // KB
+    for row in range(2):
+        for p in range(0, 4, 2):
+            for first, ref in ((p * 8, corners), (32 + p * 8, bilinear)):
+                pair = jnp.concatenate([ref[p, row].astype(F32), ref[p + 1, row].astype(F32)], axis=0)
+                table[row, first : first + 16, :columns] = pair.astype(BF16)
+        number = wedge[row] * blocks + hit[row : row + 1]
+        base[1 + row, :, :columns] = jnp.broadcast_to(number, (8, columns))
+    for side, there, who, row in sides:
+        @pl.when(there)
+        def _(side=side, who=who, row=row):
+            for copy in halo_copies(side, who, row)[2:]:
+                copy.start()
 
     def z_step(k, q):
         for xi in ((x,) if q == 0 else range(nc)):
@@ -238,7 +261,7 @@
         @pl.when(jnp.logical_not(there))
         def _(side=side, row=row):
             table_halo[side] = table[row]
-            base_halo[side] = base[row]
+            base[3 * side] = base[1 + row]
             coarse_halo[side] = coarse[...]
             vox_halo[side] = vox[row]
     up_rows()
@@ -394,10 +417,8 @@
     blocks = pixels // KB
     vox = voxels.reshape(rows_x, rows, channels)
     small = coarse.reshape(-1, channels)
-    base = wedge_ids[:, :, 0] * blocks + hit_block
-    base = jnp.pad(base, ((0, 0), (0, 1024 - cols_y))).reshape(rows_x, 8, 128)
     dma = pltpu.SemaphoreType.DMA
-    feats, onehot, up, vox_halo, base_halo = pl.pallas_call(
+    feats, onehot, up, vox_halo, base = pl.pallas_call(
         functools.partial(collect, ns, nc),
         name="collect",
         out_shape=(
@@ -405,19 +426,28 @@
             jax.ShapeDtypeStruct((4, rows, KB), BF16),
             jax.ShapeDtypeStruct((2, cols_y // 2, 2, layers, channels), F32),
             jax.ShapeDtypeStruct((2, rows, channels), BF16),
-            jax.ShapeDtypeStruct((2, 8, 128), jnp.int32),
+            jax.ShapeDtypeStruct((4, 8, 256), jnp.int32),
         ),
-        in_specs=spaces(pl.ANY, *[VMEM] * 7),
+        in_specs=spaces(*[pltpu.HBM] * 9),
         out_specs=tuple(spaces(pl.ANY, *[VMEM] * 4)),
         scratch_shapes=[
+            VMEM(vox.shape, BF16),
+            VMEM(small.shape, BF16),
+            VMEM((4, rows_x, layers, cols_y), jnp.int32),
+            VMEM((4, rows_x, layers, cols_y), BF16),
+            VMEM((rows_x, 1, cols_y), jnp.int32),
+            VMEM((rows_x, cols_y), jnp.int32),
+            VMEM((4, channels), BF16),
+            VMEM(w_up.shape, BF16),
             VMEM((2,) + small.shape, BF16),
-            VMEM((2, 8, layers, 256), F32),
-            VMEM((2, 8, layers, 256), F32),
+            VMEM((2, 8 * layers, 256), BF16),
+            VMEM((2, 8 * layers, 256), BF16),
             VMEM((2 * small.shape[0], channels), F32),
             VMEM((channels, 4 * KB), BF16),
             VMEM((rows, channels), F32),
             VMEM((rows, KB), F32),
             dma(()),
+            dma((8,)),
             dma((2, 2, ns, nc)),
             dma((2, 2, ns, nc)),
             dma((2, ns, nc)),
@@ -430,8 +460,9 @@
             collective_id=0, has_side_effects=True, vmem_limit_bytes=LIMIT
         ),
     )(image_feat.reshape(2, 2, quarter, channels), vox, small,
-      jnp.swapaxes(corners, 2, 3), jnp.swapaxes(bilinear, 2, 3), base, w_point.T, w_up)
-    index = jnp.concatenate([base_halo[:1], base, base_halo[1:]], axis=0).reshape(4, 1024)
+      jnp.swapaxes(corners, 2, 3), jnp.swapaxes(bilinear, 2, 3),
+      jnp.swapaxes(wedge_ids, 1, 2), hit_block, w_point.T, w_up)
+    index = base[:, 0]
     blocks_all = feats.reshape(ns * nc * blocks, KB, channels)
     attended, face_in = pl.pallas_call(
         functools.partial(attend, ns, nc),

time: 74.2 us -> 74.7 us (level)
  local copies, waits for them, and re-layouts: 6.6 us -> 7.97 us
    unnamed x21 -> x24, local copies, waits for them, and re-layouts: 6.59 us -> 7.95 us
where the time goes in v4:
time: 74.7 us; the launch traced here: 74.2 us
  Pallas kernels  66.2 us (89%)
  local copies, waits for them, and re-layouts  7.97 us (11%)
    pallas_call x1, Pallas kernels, body(): pl.pallas_call(functools.partial(collect, ns, nc), name='collect', out_sh...  50.1 us
    pallas_call x1, Pallas kernels, body(): pl.pallas_call(functools.partial(attend, ns, nc), name='attend', out_shap...  8.43 us
    unnamed x24, local copies, waits for them, and re-layouts  7.95 us
    pallas_call x1, Pallas kernels, body(): pl.pallas_call(convolve, name='convolve', out_shape=jax.ShapeDtypeStruct(...  7.63 us

profile of v4, /device:TPU:0, one launch (start us, length us, event | category | flops | bytes accessed | tf_op | source)
XLA Modules:
  0.0 74.2 jit_solution(3051007493991962134)
XLA Ops:
  0.0 0.0 copy-start
  0.0 1.1 %copy-done = bf16[2,200,8,128]{3,2,1,0:T(8,128)(2,1)S(1)} copy-done((bf16[2,200,8,128]{3,2,1,0:T(8,128)(2,1)S(1)}, bf16[2,200,8,128]{3,2,1,0:T(8,128)(2,1)}, u32[]{:S(2)}) %copy-start) | copy-done | bytes 819224
  1.1 0.0 copy-start.2
  1.1 1.2 %copy-done.2 = bf16[4,4,2,128,128]{4,3,2,1,0:T(8,128)(2,1)S(1)} copy-done((bf16[4,4,2,128,128]{4,3,2,1,0:T(8,128)(2,1)S(1)}, bf16[4,4,2,128,128]{4,3,2,1,0:T(8,128)(2,1)}, u32[]{:S(2)}) %copy-start.2) | copy-done | bytes 1048600
  2.4 0.0 copy-start.4
  2.4 1.0 %copy-done.4 = bf16[2048,128]{1,0:T(8,128)(2,1)S(1)} copy-done((bf16[2048,128]{1,0:T(8,128)(2,1)S(1)}, bf16[2048,128]{1,0:T(8,128)(2,1)}, u32[]{:S(2)}) %copy-start.4) | copy-done | bytes 524312
  3.4 0.0 copy-start.5
  3.4 0.9 %copy-done.5 = bf16[1,100,4,128]{3,2,1,0:T(4,128)(2,1)S(1)} copy-done((bf16[1,100,4,128]{3,2,1,0:T(4,128)(2,1)S(1)}, bf16[1,100,4,128]{3,2,1,0:T(4,128)(2,1)}, u32[]{:S(2)}) %copy-start.5) | copy-done | bytes 102424
  4.3 0.0 copy-start.6
  4.3 0.8 %copy-done.6 = s32[4,2,200,8]{2,3,1,0:T(8,128)S(1)} copy-done((s32[4,2,200,8]{2,3,1,0:T(8,128)S(1)}, s32[4,2,200,8]{2,3,1,0:T(8,128)}, u32[]{:S(2)}) %copy-start.6) | copy-done | bytes 51224
  5.1 0.0 copy-start.7
  5.2 0.8 %copy-done.7 = bf16[4,2,200,8]{2,3,1,0:T(8,128)(2,1)S(1)} copy-done((bf16[4,2,200,8]{2,3,1,0:T(8,128)(2,1)S(1)}, bf16[4,2,200,8]{2,3,1,0:T(8,128)(2,1)}, u32[]{:S(2)}) %copy-start.7) | copy-done | bytes 25624
  5.9 0.0 copy-start.9
  5.9 0.7 copy-done.9
  6.6 0.0 copy-start.10
  6.6 0.7 copy-done.10
  7.3 0.0 copy-start.11
  7.3 0.7 copy-done.11
  8.0 0.0 copy-start.1
  8.0 0.0 copy-start.8
  8.0 50.1 %collect.1 = (bf16[4,2,2,2,512,128]{5,4,3,2,1,0:T(8,128)(2,1)S(1)}, bf16[4,1600,128]{2,1,0:T(8,128)(2,1)S(1)}, f32[2,100,2,8,128]{4,3,2,1,0:T(8,128)S(1)}, bf16[...) custom-call(bf16[2,2,512,128]{3,2,1,0:T(8,128)(2,1)S(1)} %bitcast.17, bf16[2,1600,128]{2,1,0:T(8,128)(2,1)S(1)} %bitcast.13, ...), custom_call_target="tpu_custom_call" | custom-call | tf_op jit(solution)/shard_map/collect/pallas_call | solution.py:421
  58.1 0.0 copy-done.1
  58.1 0.0 copy-done.8
  58.1 0.0 copy-start.3
  58.1 8.4 %attend.1 = (bf16[4,1600,128]{2,1,0:T(8,128)(2,1)S(1)}, bf16[4,208,128]{2,1,0:T(8,128)(2,1)S(1)}) custom-call(s32[4,256]{1,0:T(4,128)S(1)} %slice_bitcast_fusion.base, bf16[128,128,128]{2,1,0:T(8,128)(2,1)S(1)} %bitcast.12, bf16[4,1600,128]{2,1,0:T(8,128)(2,1)S(1)} %get-tuple-element.14.onehot, bf16[2,1600,128]{2,1,0:T(8,128)(2,1)S(1)} %bitcast.14, ...), custom_call_target="tpu_custom_call" | custom-call | tf_op jit(solution)/shard_map/attend/pallas_call | solution.py:467
  66.6 0.0 copy-done.3
  66.6 7.6 %convolve.1 = bf16[2,200,8,128]{3,2,1,0:T(8,128)(2,1)} custom-call(bf16[4,1600,128]{2,1,0:T(8,128)(2,1)S(1)} %get-tuple-element.16.attended, bf16[4,208,128]{2,1,0:T(8,128)(2,1)S(1)} %get-tuple-element.17.face_in, f32[2,1600,128]{2,1,0:T(8,128)S(1)} %bitcast.15, bf16[3,3,384,128]{3,2,1,0:T(8,128)(2,1)S(1)} %bitcast.16), custom_call_target="tpu_custom_call" | custom-call | tf_op jit(solution)/shard_map/convolve/pallas_call | solution.py:487
  (2 shorter events, 0.0 us)
Async XLA Ops:
  0.0 1.1 %copy-start = (bf16[2,200,8,128]{3,2,1,0:T(8,128)(2,1)S(1)}, bf16[2,200,8,128]{3,2,1,0:T(8,128)(2,1)}, u32[]{:S(2)}) copy-start(bf16[2,200,8,128]{3,2,1,0:T(8,128)(2,1)} %param.11) | copy-start | bytes 2457604
  1.1 1.2 %copy-start.2 = (bf16[4,4,2,128,128]{4,3,2,1,0:T(8,128)(2,1)S(1)}, bf16[4,4,2,128,128]{4,3,2,1,0:T(8,128)(2,1)}, u32[]{:S(2)}) copy-start(bf16[4,4,2,128,128]{4,3,2,1,0:T(8,128)(2,1)} %up_hbm.1) | copy-start | bytes 3145732
  2.4 1.0 %copy-start.4 = (bf16[2048,128]{1,0:T(8,128)(2,1)S(1)}, bf16[2048,128]{1,0:T(8,128)(2,1)}, u32[]{:S(2)}) copy-start(bf16[2048,128]{1,0:T(8,128)(2,1)} %param.12) | copy-start | bytes 1572868
  3.4 0.9 %copy-start.5 = (bf16[1,100,4,128]{3,2,1,0:T(4,128)(2,1)S(1)}, bf16[1,100,4,128]{3,2,1,0:T(4,128)(2,1)}, u32[]{:S(2)}) copy-start(bf16[1,100,4,128]{3,2,1,0:T(4,128)(2,1)} %param.13) | copy-start | bytes 307204
  4.3 0.8 %copy-start.6 = (s32[4,2,200,8]{2,3,1,0:T(8,128)S(1)}, s32[4,2,200,8]{2,3,1,0:T(8,128)}, u32[]{:S(2)}) copy-start(s32[4,2,200,8]{2,3,1,0:T(8,128)} %param.16) | copy-start | bytes 153604
  5.1 0.8 %copy-start.7 = (bf16[4,2,200,8]{2,3,1,0:T(8,128)(2,1)S(1)}, bf16[4,2,200,8]{2,3,1,0:T(8,128)(2,1)}, u32[]{:S(2)}) copy-start(bf16[4,2,200,8]{2,3,1,0:T(8,128)(2,1)} %param.17) | copy-start | bytes 76804
  5.9 0.7 copy-start.9
  6.6 0.7 copy-start.10
  7.3 0.7 copy-start.11
  8.0 50.1 %copy-start.1 = (bf16[2,200,8,128]{3,2,1,0:T(8,128)(2,1)S(1)}, bf16[2,200,8,128]{3,2,1,0:T(8,128)(2,1)}, u32[]{:S(2)}) copy-start(bf16[2,200,8,128]{3,2,1,0:T(8,128)(2,1)} %param.11) | copy-start | bytes 2457604
  8.0 50.2 %copy-start.8 = (bf16[128,128]{1,0:T(8,128)(2,1)S(1)}, bf16[128,128]{1,0:T(8,128)(2,1)}, u32[]{:S(2)}) copy-start(bf16[128,128]{1,0:T(8,128)(2,1)} %w_out.1) | copy-start | bytes 98308
  58.1 8.5 %copy-start.3 = (bf16[3,3,3,128,128]{4,3,2,1,0:T(8,128)(2,1)S(1)}, bf16[3,3,3,128,128]{4,3,2,1,0:T(8,128)(2,1)}, u32[]{:S(2)}) copy-start(bf16[3,3,3,128,128]{4,3,2,1,0:T(8,128)(2,1)} %param.20) | copy-start | bytes 2654212
